TPU v7x, 128 devices: a whole 4x4x4 slice. The times are simulated.
128 devices in a mesh: row: 16 (over x, y_lo, core), col: 8 (over y_hi, z).
Axes of the slice: x: 4, y: 4 (y_hi: 2, y_lo: 2; y = y_hi * 2 + y_lo), z: 4, core: 2. Of those that a mesh axis runs over, the one named last changes fastest.
Arguments:
- features: bfloat16 [65536, 256], P(('row', 'col')), may hold values from -6 to 6
- weight: bfloat16 [256, 256], replicated, may hold values from -0.375 to 0.375
- cotangent: bfloat16 [65536, 256], P(('col', 'row')), may hold values from -6 to 6
- block_rows: int32 [16, 8, 384], P('row', 'col'), may hold values from 0 to 63
- block_cols: int32 [16, 8, 384], P('row', 'col'), may hold values from 0 to 31
- counts: int32 [16, 8], P('row', 'col'), may hold values from 64 to 384, as said below
- values: bfloat16 [16, 8, 384, 128, 128], P('row', 'col'), may hold values from -0.078125 to 0.078125
Outputs:
- output: bfloat16 [65536, 256], P(('col', 'row'))
- grad_weight: float32 [256, 256], replicated
- grad_features: bfloat16 [65536, 256], P(('row', 'col'))
Inputs may be any that keep to these rules, and one draw needn't show every extreme that they name: `counts`: at least one tile holds 384 blocks.
All inputs are finite; a program needn't handle non-finite values.
Results may differ from a plain program's by a relative error of at most 0.0049.
Values may be sent and summed in bfloat16 or wider, within the bound.
A program may use at most 128 MiB of HBM per device.

v0:
```python
import jax
import jax.numpy as jnp
from jax import lax
from jax.sharding import PartitionSpec as P

BLOCK = 128
GROUP = 64


def block_product(tile_values, out_index, in_index, count, source, out_first, out_count, flipped):
    width = source.shape[-1]
    block = tile_values.shape[-1]
    source_blocks = source.reshape(-1, block, width)
    in_blocks = source_blocks.shape[0]
    form = "kji,kjf->kif" if flipped else "kij,kjf->kif"
    in_labels = jnp.arange(in_blocks, dtype=jnp.int32)
    out_labels = jnp.arange(out_count, dtype=jnp.int32)

    def advance(index, total):
        start = index * GROUP
        pieces = lax.dynamic_slice_in_dim(tile_values, start, GROUP, 0)
        target = lax.dynamic_slice_in_dim(out_index, start, GROUP, 0) - out_first
        anchor = lax.dynamic_slice_in_dim(in_index, start, GROUP, 0)
        active = start + jnp.arange(GROUP, dtype=jnp.int32) < count
        active = active & (target >= 0) & (target < out_count)
        pick_table = (anchor[:, None] == in_labels[None, :]).astype(jnp.bfloat16)
        picked = jnp.einsum(
            "ko,obf->kbf", pick_table, source_blocks, preferred_element_type=jnp.float32
        ).astype(jnp.bfloat16)
        product = jnp.einsum(form, pieces, picked, preferred_element_type=jnp.float32)
        place_table = ((target[:, None] == out_labels[None, :]) & active[:, None]).astype(
            jnp.float32
        )
        return total + jnp.einsum(
            "ko,kif->oif", place_table, product, precision=lax.Precision.HIGHEST
        )

    total = jnp.zeros((out_count, block, width), jnp.float32)
    total = lax.fori_loop(0, tile_values.shape[0] // GROUP, advance, total)
    return total.reshape(out_count * block, width)


def body(features, weight, cotangent, block_rows, block_cols, counts, values):
    grid_rows = lax.axis_size("row")
    grid_cols = lax.axis_size("col")
    tile_values = values[0, 0]
    tile_rows = block_rows[0, 0]
    tile_cols = block_cols[0, 0]
    count = counts[0, 0]
    local_blocks = features.shape[0] // BLOCK
    nodes = local_blocks * BLOCK * grid_rows * grid_cols
    panel = lax.all_gather(features, "col", axis=0, tiled=True)
    partial_sums = block_product(
        tile_values, tile_rows, tile_cols, count, panel, 0, local_blocks * grid_rows, False
    )
    aggregate = lax.psum_scatter(partial_sums, "row", scatter_dimension=0, tiled=True).astype(
        jnp.bfloat16
    )
    output = jnp.dot(aggregate, weight, preferred_element_type=jnp.float32).astype(jnp.bfloat16)
    weight_term = jnp.dot(aggregate.T, cotangent, preferred_element_type=jnp.float32)
    grad_local = jnp.dot(cotangent, weight.T, preferred_element_type=jnp.float32).astype(
        jnp.bfloat16
    )
    grad_slab = lax.all_gather(grad_local, "row", axis=0, tiled=True)
    back_sums = block_product(
        tile_values, tile_cols, tile_rows, count, grad_slab, 0, local_blocks * grid_cols, True
    )
    grad_features = lax.psum_scatter(back_sums, "col", scatter_dimension=0, tiled=True)
    weight_total = lax.psum(weight_term, ("row", "col"))
    grad_weight = weight_total * float(nodes) ** (-0.5)
    return (output, grad_weight, grad_features.astype(jnp.bfloat16))


def solution(mesh):
    placed = (
        P(("row", "col"), None),
        P(),
        P(("col", "row"), None),
        P("row", "col", None),
        P("row", "col", None),
        P("row", "col"),
        P("row", "col", None, None, None),
    )
    return jax.shard_map(
        body,
        mesh=mesh,
        in_specs=placed,
        out_specs=(P(("col", "row"), None), P(), P(("row", "col"), None)),
        check_vma=False,
    )
```

profile of v0, /device:TPU:1, one launch (start us, length us, event | category | flops | bytes accessed | tf_op | source)
XLA Modules:
  0.0 674.8 jit_solution(3675447191912231820)
XLA Ops:
  12.2 39.0 %all-gather.5.cloned.1.call-done = bf16[8192,256]{1,0:T(8,128)(2,1)} async-done(((bf16[512,256]{1,0:T(8,128)(2,1)}), bf16[8192,256]{1,0:T(8,128)(2,1)}) %all-gather.5.cloned.1.call-update) | async-done | bytes 4194320 | tf_op jit(solution)/shard_map/all_gather | solution.py:64
  51.3 172.5 %while.29 = (s32[]{:T(128)}, f32[32,128,256]{2,0,1:T(8,128)}, s32[384]{0:T(512)S(1)}, s32[]{:T(128)}, bf16[384,128,128]{2,1,0:T(8,128)(2,1)}, /*index=5*/s32[384...) while((s32[]{:T(128)}, f32[32,128,256]{2,0,1:T(8,128)}, ...), condition=%wide.region_5.0_spmd.clone, body=%wide.region_4.0_spmd.clone.sunk | while | flops 1612718464 | bytes 39847736 | solution.py:39
  51.3 5.5 fusion.75
  56.8 8.2 %fusion.76 = f32[64,128,256]{2,1,0:T(8,128)} fusion(bf16[64,128,256]{2,0,1:T(8,128)(2,1)S(1)} %fusion.75, bf16[384,128,128]{2,1,0:T(8,128)(2,1)} %get-tuple-element.554, s32[]{:T(128)S(6)} %select_n.23), kind=kOutput, calls=%fused_computation.25.clone.1 | convolution fusion | flops 536870912 | bytes 14680068 | tf_op jit(solution)/shard_map/while/body/eval_jaxpr/kji,kjf->kif/dot_general | solution.py:30
  65.7 13.2 %select_add_fusion.5 = f32[32,128,256]{2,0,1:T(8,128)} fusion(f32[32,128,256]{2,0,1:T(8,128)} %get-tuple-element.540, f32[64,128,256]{2,1,0:T(8,128)} %fusion.76, pred[]{:T(512)S(6)} %compare.7, s32[64]{0:T(128)S(1)} %get-tuple-element.493, pred[64]{0:T(512)(128)(4,1)S(1)} %get-tuple-element.494), kind=kOutput, calls=%fused_computation.28.clone.1 | convolution fusion | flops 807407616 | bytes 16777536 | tf_op jit(solution)/shard_map/while/body/eval_jaxpr/ko,kif->oif/dot_general | solution.py:34
  84.5 8.3 %fusion.76 = f32[64,128,256]{2,1,0:T(8,128)} fusion(bf16[64,128,256]{2,0,1:T(8,128)(2,1)S(1)} %fusion.75, bf16[384,128,128]{2,1,0:T(8,128)(2,1)} %get-tuple-element.554, s32[]{:T(128)S(6)} %select_n.23), kind=kOutput, calls=%fused_computation.25.clone.1 | convolution fusion | flops 536870912 | bytes 14680068 | tf_op jit(solution)/shard_map/while/body/eval_jaxpr/kji,kjf->kif/dot_general | solution.py:30
  93.5 14.5 %select_add_fusion.5 = f32[32,128,256]{2,0,1:T(8,128)} fusion(f32[32,128,256]{2,0,1:T(8,128)} %get-tuple-element.540, f32[64,128,256]{2,1,0:T(8,128)} %fusion.76, pred[]{:T(512)S(6)} %compare.7, s32[64]{0:T(128)S(1)} %get-tuple-element.493, pred[64]{0:T(512)(128)(4,1)S(1)} %get-tuple-element.494), kind=kOutput, calls=%fused_computation.28.clone.1 | convolution fusion | flops 807407616 | bytes 16777536 | tf_op jit(solution)/shard_map/while/body/eval_jaxpr/ko,kif->oif/dot_general | solution.py:34
  113.5 8.2 %fusion.76 = f32[64,128,256]{2,1,0:T(8,128)} fusion(bf16[64,128,256]{2,0,1:T(8,128)(2,1)S(1)} %fusion.75, bf16[384,128,128]{2,1,0:T(8,128)(2,1)} %get-tuple-element.554, s32[]{:T(128)S(6)} %select_n.23), kind=kOutput, calls=%fused_computation.25.clone.1 | convolution fusion | flops 536870912 | bytes 14680068 | tf_op jit(solution)/shard_map/while/body/eval_jaxpr/kji,kjf->kif/dot_general | solution.py:30
  122.4 14.4 %select_add_fusion.5 = f32[32,128,256]{2,0,1:T(8,128)} fusion(f32[32,128,256]{2,0,1:T(8,128)} %get-tuple-element.540, f32[64,128,256]{2,1,0:T(8,128)} %fusion.76, pred[]{:T(512)S(6)} %compare.7, s32[64]{0:T(128)S(1)} %get-tuple-element.493, pred[64]{0:T(512)(128)(4,1)S(1)} %get-tuple-element.494), kind=kOutput, calls=%fused_computation.28.clone.1 | convolution fusion | flops 807407616 | bytes 16777536 | tf_op jit(solution)/shard_map/while/body/eval_jaxpr/ko,kif->oif/dot_general | solution.py:34
  142.3 8.2 %fusion.76 = f32[64,128,256]{2,1,0:T(8,128)} fusion(bf16[64,128,256]{2,0,1:T(8,128)(2,1)S(1)} %fusion.75, bf16[384,128,128]{2,1,0:T(8,128)(2,1)} %get-tuple-element.554, s32[]{:T(128)S(6)} %select_n.23), kind=kOutput, calls=%fused_computation.25.clone.1 | convolution fusion | flops 536870912 | bytes 14680068 | tf_op jit(solution)/shard_map/while/body/eval_jaxpr/kji,kjf->kif/dot_general | solution.py:30
  151.2 14.4 %select_add_fusion.5 = f32[32,128,256]{2,0,1:T(8,128)} fusion(f32[32,128,256]{2,0,1:T(8,128)} %get-tuple-element.540, f32[64,128,256]{2,1,0:T(8,128)} %fusion.76, pred[]{:T(512)S(6)} %compare.7, s32[64]{0:T(128)S(1)} %get-tuple-element.493, pred[64]{0:T(512)(128)(4,1)S(1)} %get-tuple-element.494), kind=kOutput, calls=%fused_computation.28.clone.1 | convolution fusion | flops 807407616 | bytes 16777536 | tf_op jit(solution)/shard_map/while/body/eval_jaxpr/ko,kif->oif/dot_general | solution.py:34
  171.2 8.2 %fusion.76 = f32[64,128,256]{2,1,0:T(8,128)} fusion(bf16[64,128,256]{2,0,1:T(8,128)(2,1)S(1)} %fusion.75, bf16[384,128,128]{2,1,0:T(8,128)(2,1)} %get-tuple-element.554, s32[]{:T(128)S(6)} %select_n.23), kind=kOutput, calls=%fused_computation.25.clone.1 | convolution fusion | flops 536870912 | bytes 14680068 | tf_op jit(solution)/shard_map/while/body/eval_jaxpr/kji,kjf->kif/dot_general | solution.py:30
  180.1 14.4 %select_add_fusion.5 = f32[32,128,256]{2,0,1:T(8,128)} fusion(f32[32,128,256]{2,0,1:T(8,128)} %get-tuple-element.540, f32[64,128,256]{2,1,0:T(8,128)} %fusion.76, pred[]{:T(512)S(6)} %compare.7, s32[64]{0:T(128)S(1)} %get-tuple-element.493, pred[64]{0:T(512)(128)(4,1)S(1)} %get-tuple-element.494), kind=kOutput, calls=%fused_computation.28.clone.1 | convolution fusion | flops 807407616 | bytes 16777536 | tf_op jit(solution)/shard_map/while/body/eval_jaxpr/ko,kif->oif/dot_general | solution.py:34
  200.1 8.2 %fusion.76 = f32[64,128,256]{2,1,0:T(8,128)} fusion(bf16[64,128,256]{2,0,1:T(8,128)(2,1)S(1)} %fusion.75, bf16[384,128,128]{2,1,0:T(8,128)(2,1)} %get-tuple-element.554, s32[]{:T(128)S(6)} %select_n.23), kind=kOutput, calls=%fused_computation.25.clone.1 | convolution fusion | flops 536870912 | bytes 14680068 | tf_op jit(solution)/shard_map/while/body/eval_jaxpr/kji,kjf->kif/dot_general | solution.py:30
  208.9 14.4 %select_add_fusion.5 = f32[32,128,256]{2,0,1:T(8,128)} fusion(f32[32,128,256]{2,0,1:T(8,128)} %get-tuple-element.540, f32[64,128,256]{2,1,0:T(8,128)} %fusion.76, pred[]{:T(512)S(6)} %compare.7, s32[64]{0:T(128)S(1)} %get-tuple-element.493, pred[64]{0:T(512)(128)(4,1)S(1)} %get-tuple-element.494), kind=kOutput, calls=%fused_computation.28.clone.1 | convolution fusion | flops 807407616 | bytes 16777536 | tf_op jit(solution)/shard_map/while/body/eval_jaxpr/ko,kif->oif/dot_general | solution.py:34
  223.8 6.6 copy.12
  230.4 179.7 %while.28 = (s32[]{:T(128)}, f32[64,128,256]{2,0,1:T(8,128)}, s32[384]{0:T(512)S(1)}, s32[]{:T(128)}, bf16[384,128,128]{2,1,0:T(8,128)(2,1)}, /*index=5*/s32[384...) while((s32[]{:T(128)}, f32[64,128,256]{2,0,1:T(8,128)}, ...), condition=%wide.region_1.0_spmd.clone, body=%wide.region_0.0_spmd.clone.sunk | while | flops 2285906432 | bytes 46139192 | solution.py:39
  233.6 7.8 %fusion.69 = f32[64,128,256]{2,1,0:T(8,128)} fusion(bf16[64,128,256]{2,0,1:T(8,128)(2,1)S(1)} %fusion.68, bf16[384,128,128]{2,1,0:T(8,128)(2,1)} %get-tuple-element.521, s32[]{:T(128)S(6)} %select_n.22), kind=kOutput, calls=%fused_computation.8.clone.1 | convolution fusion | flops 536870912 | bytes 14680068 | tf_op jit(solution)/shard_map/while/body/eval_jaxpr/kij,kjf->kif/dot_general | solution.py:30
  242.1 16.2 %select_add_fusion.4 = f32[64,128,256]{2,0,1:T(8,128)} fusion(f32[64,128,256]{2,0,1:T(8,128)} %get-tuple-element.507, pred[]{:T(512)S(6)} %compare.6, f32[64,128,256]{2,1,0:T(8,128)} %fusion.69, s32[64]{0:T(128)S(1)} %get-tuple-element.484, pred[64]{0:T(512)(128)(4,1)S(1)} %get-tuple-element.485), kind=kOutput, calls=%fused_computation.7.clone.1 | convolution fusion | flops 1614815232 | bytes 25166144 | tf_op jit(solution)/shard_map/while/body/eval_jaxpr/ko,kif->oif/dot_general | solution.py:34
  261.5 7.9 %fusion.69 = f32[64,128,256]{2,1,0:T(8,128)} fusion(bf16[64,128,256]{2,0,1:T(8,128)(2,1)S(1)} %fusion.68, bf16[384,128,128]{2,1,0:T(8,128)(2,1)} %get-tuple-element.521, s32[]{:T(128)S(6)} %select_n.22), kind=kOutput, calls=%fused_computation.8.clone.1 | convolution fusion | flops 536870912 | bytes 14680068 | tf_op jit(solution)/shard_map/while/body/eval_jaxpr/kij,kjf->kif/dot_general | solution.py:30
  270.1 18.6 %select_add_fusion.4 = f32[64,128,256]{2,0,1:T(8,128)} fusion(f32[64,128,256]{2,0,1:T(8,128)} %get-tuple-element.507, pred[]{:T(512)S(6)} %compare.6, f32[64,128,256]{2,1,0:T(8,128)} %fusion.69, s32[64]{0:T(128)S(1)} %get-tuple-element.484, pred[64]{0:T(512)(128)(4,1)S(1)} %get-tuple-element.485), kind=kOutput, calls=%fused_computation.7.clone.1 | convolution fusion | flops 1614815232 | bytes 25166144 | tf_op jit(solution)/shard_map/while/body/eval_jaxpr/ko,kif->oif/dot_general | solution.py:34
  291.9 7.8 %fusion.69 = f32[64,128,256]{2,1,0:T(8,128)} fusion(bf16[64,128,256]{2,0,1:T(8,128)(2,1)S(1)} %fusion.68, bf16[384,128,128]{2,1,0:T(8,128)(2,1)} %get-tuple-element.521, s32[]{:T(128)S(6)} %select_n.22), kind=kOutput, calls=%fused_computation.8.clone.1 | convolution fusion | flops 536870912 | bytes 14680068 | tf_op jit(solution)/shard_map/while/body/eval_jaxpr/kij,kjf->kif/dot_general | solution.py:30
  300.5 18.6 %select_add_fusion.4 = f32[64,128,256]{2,0,1:T(8,128)} fusion(f32[64,128,256]{2,0,1:T(8,128)} %get-tuple-element.507, pred[]{:T(512)S(6)} %compare.6, f32[64,128,256]{2,1,0:T(8,128)} %fusion.69, s32[64]{0:T(128)S(1)} %get-tuple-element.484, pred[64]{0:T(512)(128)(4,1)S(1)} %get-tuple-element.485), kind=kOutput, calls=%fused_computation.7.clone.1 | convolution fusion | flops 1614815232 | bytes 25166144 | tf_op jit(solution)/shard_map/while/body/eval_jaxpr/ko,kif->oif/dot_general | solution.py:34
  322.3 7.8 %fusion.69 = f32[64,128,256]{2,1,0:T(8,128)} fusion(bf16[64,128,256]{2,0,1:T(8,128)(2,1)S(1)} %fusion.68, bf16[384,128,128]{2,1,0:T(8,128)(2,1)} %get-tuple-element.521, s32[]{:T(128)S(6)} %select_n.22), kind=kOutput, calls=%fused_computation.8.clone.1 | convolution fusion | flops 536870912 | bytes 14680068 | tf_op jit(solution)/shard_map/while/body/eval_jaxpr/kij,kjf->kif/dot_general | solution.py:30
  330.8 18.6 %select_add_fusion.4 = f32[64,128,256]{2,0,1:T(8,128)} fusion(f32[64,128,256]{2,0,1:T(8,128)} %get-tuple-element.507, pred[]{:T(512)S(6)} %compare.6, f32[64,128,256]{2,1,0:T(8,128)} %fusion.69, s32[64]{0:T(128)S(1)} %get-tuple-element.484, pred[64]{0:T(512)(128)(4,1)S(1)} %get-tuple-element.485), kind=kOutput, calls=%fused_computation.7.clone.1 | convolution fusion | flops 1614815232 | bytes 25166144 | tf_op jit(solution)/shard_map/while/body/eval_jaxpr/ko,kif->oif/dot_general | solution.py:34
  352.6 7.8 %fusion.69 = f32[64,128,256]{2,1,0:T(8,128)} fusion(bf16[64,128,256]{2,0,1:T(8,128)(2,1)S(1)} %fusion.68, bf16[384,128,128]{2,1,0:T(8,128)(2,1)} %get-tuple-element.521, s32[]{:T(128)S(6)} %select_n.22), kind=kOutput, calls=%fused_computation.8.clone.1 | convolution fusion | flops 536870912 | bytes 14680068 | tf_op jit(solution)/shard_map/while/body/eval_jaxpr/kij,kjf->kif/dot_general | solution.py:30
  361.1 18.6 %select_add_fusion.4 = f32[64,128,256]{2,0,1:T(8,128)} fusion(f32[64,128,256]{2,0,1:T(8,128)} %get-tuple-element.507, pred[]{:T(512)S(6)} %compare.6, f32[64,128,256]{2,1,0:T(8,128)} %fusion.69, s32[64]{0:T(128)S(1)} %get-tuple-element.484, pred[64]{0:T(512)(128)(4,1)S(1)} %get-tuple-element.485), kind=kOutput, calls=%fused_computation.7.clone.1 | convolution fusion | flops 1614815232 | bytes 25166144 | tf_op jit(solution)/shard_map/while/body/eval_jaxpr/ko,kif->oif/dot_general | solution.py:34
  382.8 7.8 %fusion.69 = f32[64,128,256]{2,1,0:T(8,128)} fusion(bf16[64,128,256]{2,0,1:T(8,128)(2,1)S(1)} %fusion.68, bf16[384,128,128]{2,1,0:T(8,128)(2,1)} %get-tuple-element.521, s32[]{:T(128)S(6)} %select_n.22), kind=kOutput, calls=%fused_computation.8.clone.1 | convolution fusion | flops 536870912 | bytes 14680068 | tf_op jit(solution)/shard_map/while/body/eval_jaxpr/kij,kjf->kif/dot_general | solution.py:30
  391.4 18.6 %select_add_fusion.4 = f32[64,128,256]{2,0,1:T(8,128)} fusion(f32[64,128,256]{2,0,1:T(8,128)} %get-tuple-element.507, pred[]{:T(512)S(6)} %compare.6, f32[64,128,256]{2,1,0:T(8,128)} %fusion.69, s32[64]{0:T(128)S(1)} %get-tuple-element.484, pred[64]{0:T(512)(128)(4,1)S(1)} %get-tuple-element.485), kind=kOutput, calls=%fused_computation.7.clone.1 | convolution fusion | flops 1614815232 | bytes 25166144 | tf_op jit(solution)/shard_map/while/body/eval_jaxpr/ko,kif->oif/dot_general | solution.py:34
  410.1 11.5 %copy.11 = f32[64,128,256]{2,1,0:T(8,128)} copy(f32[64,128,256]{2,0,1:T(8,128)} %get-tuple-element.311) | data formatting | bytes 16777216 | tf_op jit(solution)/shard_map/while | solution.py:39
  423.4 94.9 %reduce-scatter.3.cloned.1.call-done = f32[512,256]{1,0:T(8,128)} async-done(((f32[8192,256]{1,0:T(8,128)}), f32[512,256]{1,0:T(8,128)}) %reduce-scatter.3.cloned.1.call-update) | async-done | bytes 524304 | tf_op jit(solution)/shard_map/reduce_scatter | solution.py:56
  522.3 144.1 %all-reduce.2.cloned.1.call-done = f32[256,256]{1,0:T(8,128)} async-done(((f32[256,256]{1,0:T(8,128)}), f32[256,256]{1,0:T(8,128)}) %all-reduce.2.cloned.1.call-update) | async-done | bytes 262160 | tf_op jit(solution)/shard_map/psum | solution.py:69
  (60 shorter events, 68.1 us)
Async XLA Ops:
  7.2 1.0 copy-start
  7.2 44.1 %all-gather.5.cloned.1.call-start = ((), (), s32[]{:S(2)}) async-start(), calls=%async_computation.5 | async-start | bytes 4456448 | tf_op jit(solution)/shard_map/all_gather | solution.py:64
  10.0 220.4 %all-gather.3.cloned.1.call-start = ((), (), s32[]{:S(2)}) async-start(), calls=%async_computation.2 | async-start | bytes 2359296 | tf_op jit(solution)/shard_map/all_gather | solution.py:52
  10.8 410.9 %reduce-scatter.5.cloned.1.call-start = ((), (), s32[]{:S(2)}) async-start(), calls=%async_computation.6 | async-start | bytes 4718592 | tf_op jit(solution)/shard_map/reduce_scatter | solution.py:68
  230.3 288.0 %reduce-scatter.3.cloned.1.call-start = ((), (), s32[]{:S(2)}) async-start(), calls=%async_computation.3 | async-start | bytes 8912896 | tf_op jit(solution)/shard_map/reduce_scatter | solution.py:56
  421.5 98.8 %copy-start.1 = (bf16[256,256]{1,0:T(8,128)(2,1)S(1)}, bf16[256,256]{1,0:T(8,128)(2,1)}, u32[]{:S(2)}) copy-start(bf16[256,256]{1,0:T(8,128)(2,1)} %param.12) | copy-start | bytes 393220
  421.6 244.8 %all-reduce.2.cloned.1.call-start = ((), (), s32[]{:S(2)}) async-start(), calls=%async_computation.4 | async-start | bytes 524288 | tf_op jit(solution)/shard_map/psum | solution.py:69
Sparse Core Ops, SparseCore 0:
  10.3 40.9 all-gather.4
  53.6 53.4 all-gather.2
  230.5 83.2 reduce-scatter.4
  421.7 96.5 reduce-scatter.2
  524.2 142.1 all-reduce.1
where the time goes:
time: 686 us; the launch traced here: 675 us
  matrix products  348 us (51%)
  waiting for transfers between devices  279 us (41%)
  local copies, waits for them, and re-layouts  19.8 us (3%)
  between operations  14 us (2%)
  other arithmetic  13.5 us (2%)
    dot_general x12, matrix products, advance(): jnp.einsum('ko,kif->oif', place_table, product, precision=lax.Precision.H...  195 us
    psum x1, waiting for transfers between devices, body(): weight_total = lax.psum(weight_term, ('row', 'col'))  144 us
    dot_general x12, matrix products, advance(): jnp.einsum(form, pieces, picked, preferred_element_type=jnp.float32)  96 us
    reduce_scatter x1, waiting for transfers between devices, body(): lax.psum_scatter(partial_sums, 'row', scatter_dimension=0, tiled=True)  94.9 us
    dot_general x12, matrix products, advance(): jnp.einsum('ko,obf->kbf', pick_table, source_blocks, preferred_element_ty...  51.4 us
    all_gather x1, waiting for transfers between devices, body(): grad_slab = lax.all_gather(grad_local, 'row', axis=0, tiled=True)  39 us
    while x2, local copies, waits for them, and re-layouts, block_product(): total = lax.fori_loop(0, tile_values.shape[0] // GROUP, advance, total)  18 us
  transfers between devices with their start and end apart: 5, of which 3 were waited for; matrix products, arithmetic and copies ran while one was open for 56% of the time, Pallas kernels for 0%

commit v1 on v0

v1 whole, which is shorter than its diff:
```python
import functools

import jax
import jax.numpy as jnp
from jax import lax
from jax.experimental import pallas as pl
from jax.experimental.pallas import tpu as pltpu
from jax.sharding import PartitionSpec as P

MESH = pl.DeviceIdType.MESH
BF = jnp.bfloat16
F32 = jnp.float32
B = 128
NNZ = 384
SLOTS = 512
F_PAIRS = 224
B_PAIRS = 208
CHUNK = 4


def meta_kernel(rows_ref, cols_ref, count_ref, blk_f, src_f, keep_f, end_f, has_f, blk_b, src_b, keep_b, end_b, has_b):
    count = count_ref[0, 0]
    lane_k = lax.broadcasted_iota(jnp.int32, (1, NNZ), 1)
    valid = lane_k < count
    rows = jnp.where(valid, rows_ref[...], 900).astype(F32)
    cols = jnp.where(valid, cols_ref[...], 900).astype(F32)
    rows_t = jnp.transpose(jnp.broadcast_to(rows, (B, NNZ)))
    cols_t = jnp.transpose(jnp.broadcast_to(cols, (B, NNZ)))
    sub_k = lax.broadcasted_iota(jnp.int32, (NNZ, B), 0).astype(F32)
    lane_r = lax.broadcasted_iota(jnp.int32, (NNZ, B), 1).astype(F32)
    sub_kk = lax.broadcasted_iota(jnp.int32, (NNZ, NNZ), 0)
    lane_kk = lax.broadcasted_iota(jnp.int32, (NNZ, NNZ), 1)
    sub_r = lax.broadcasted_iota(jnp.int32, (B, NNZ), 0).astype(F32)
    sub_q = lax.broadcasted_iota(jnp.int32, (B, B), 0)
    lane_q = lax.broadcasted_iota(jnp.int32, (B, B), 1)

    def half_up(n):
        return ((n.astype(jnp.int32) + 1) >> 1).astype(F32)

    def one(key, key_t, src_t, blk, src, keep, end, has):
        key_tt = jnp.concatenate([key_t] * (NNZ // B), axis=1)
        same = (key_tt == jnp.broadcast_to(key, (NNZ, NNZ))) & (sub_kk < lane_kk)
        within = jnp.sum(jnp.where(same, 1.0, 0.0), axis=0, keepdims=True)
        n_l = jnp.sum(jnp.where(key_t == lane_r, 1.0, 0.0), axis=0, keepdims=True)
        hot = jnp.where(sub_r == jnp.broadcast_to(key, (B, NNZ)), 1.0, 0.0)
        n_s = jnp.sum(hot, axis=1, keepdims=True)
        q_l = half_up(n_l)
        q_s = half_up(n_s)
        s_l = jnp.sum(jnp.where(sub_q < lane_q, jnp.broadcast_to(q_s, (B, B)), 0.0), axis=0, keepdims=True)
        s_s = jnp.sum(jnp.where(lane_q < sub_q, jnp.broadcast_to(q_l, (B, B)), 0.0), axis=1, keepdims=True)
        slot = 2.0 * jnp.sum(hot * s_s, axis=0, keepdims=True) + within
        slot = jnp.where(valid, slot, 9000.0)
        slot_t = jnp.transpose(jnp.broadcast_to(slot, (B, NNZ)))
        src_clean = jnp.where(src_t < 800.0, src_t, 0.0)
        for part in range(SLOTS // B):
            match = slot_t == lane_r + float(part * B)
            found = jnp.sum(jnp.where(match, sub_k + 1.0, 0.0), axis=0, keepdims=True)
            where = jnp.sum(jnp.where(match, src_clean, 0.0), axis=0, keepdims=True)
            found = jnp.where(found == 0.0, float(NNZ + 1), found) - 1.0
            blk[:, pl.ds(part * B, B)] = found.astype(jnp.int32)
            src[:, pl.ds(part * B, B)] = where.astype(jnp.int32)
        for part in range(2):
            first = (s_s == (lane_q + part * B).astype(F32)) & (n_s > 0.0)
            starts = jnp.sum(jnp.where(first, 1.0, 0.0), axis=0, keepdims=True)
            keep[:, pl.ds(part * B, B)] = (1.0 - starts).astype(jnp.int32)
        ends = jnp.where(n_l > 0.0, s_l + q_l - 1.0, 0.0)
        end[...] = ends.astype(jnp.int32)
        has[...] = jnp.where(n_l > 0.0, 1.0, 0.0).astype(jnp.int32)

    one(rows, rows_t, cols_t, blk_f, src_f, keep_f, end_f, has_f)
    one(cols, cols_t, rows_t, blk_b, src_b, keep_b, end_b, has_b)


def build_meta(block_rows, block_cols, counts):
    shapes = [(1, SLOTS), (1, SLOTS), (1, 2 * B), (1, B), (1, B)] * 2
    return pl.pallas_call(
        meta_kernel,
        out_shape=[jax.ShapeDtypeStruct(shape, jnp.int32) for shape in shapes],
        in_specs=[
            pl.BlockSpec(memory_space=pltpu.VMEM),
            pl.BlockSpec(memory_space=pltpu.VMEM),
            pl.BlockSpec(memory_space=pltpu.SMEM),
        ],
        out_specs=[pl.BlockSpec(memory_space=pltpu.VMEM)] * 10,
    )(block_rows, block_cols, counts)


class Ring:
    def __init__(self, i, j, slot, device):
        self.i, self.j, self.slot, self.device = i, j, slot, device

    def at(self, di, dj):
        i = (self.i + di + 4) % 4
        j = self.j if dj == 0 else 1 - self.j
        return self.slot(i, j)

    def dev(self, di, dj):
        i = (self.i + di + 4) % 4
        j = self.j if dj == 0 else 1 - self.j
        return self.device(i, j)


def remote(src, dst, send, recv, index, device):
    return pltpu.make_async_remote_copy(
        src_ref=src, dst_ref=dst, send_sem=send.at[index], recv_sem=recv.at[index], device_id=device, device_id_type=MESH
    )


def gather_steps(buf, ring, send, recv, arrived):
    def part(slot, half):
        return buf.at[pl.ds(slot * CHUNK + 2 * half, 2)]

    right, left, mate = ring.dev(1, 0), ring.dev(-1, 0), ring.dev(0, 1)
    started = []

    def go(index, slot, half, device):
        copy = remote(part(slot, half), part(slot, half), send, recv, index, device)
        copy.start()
        started.append(copy)

    def come(index, slot, half):
        remote(part(slot, half), part(slot, half), send, recv, index, right).wait_recv()
        arrived(slot, half)

    own, other = ring.at(0, 0), ring.at(0, 1)
    go(0, own, 0, mate)
    go(2, own, 0, right)
    go(8, own, 1, left)
    go(1, own, 1, mate)
    go(3, own, 1, right)
    go(9, own, 0, left)
    arrived(own, 0)
    arrived(own, 1)
    yield
    come(2, ring.at(-1, 0), 0)
    go(6, ring.at(-1, 0), 0, right)
    yield
    come(8, ring.at(1, 0), 1)
    go(12, ring.at(1, 0), 1, left)
    yield
    come(0, other, 0)
    go(4, other, 0, right)
    go(11, other, 0, left)
    yield
    come(1, other, 1)
    go(10, other, 1, left)
    go(5, other, 1, right)
    yield
    come(3, ring.at(-1, 0), 1)
    come(9, ring.at(1, 0), 0)
    yield
    come(4, ring.at(-1, 1), 0)
    go(7, ring.at(-1, 1), 0, right)
    yield
    come(10, ring.at(1, 1), 1)
    go(13, ring.at(1, 1), 1, left)
    yield
    come(6, ring.at(-2, 0), 0)
    come(12, ring.at(2, 0), 1)
    yield
    come(5, ring.at(-1, 1), 1)
    come(11, ring.at(1, 1), 0)
    yield
    come(7, ring.at(-2, 1), 0)
    come(13, ring.at(2, 1), 1)
    for copy in started:
        copy.wait_send()


def scatter_steps(buf, ring, send, recv, relay_l, relay_r, from_l, from_r, from_mate, ready, finish):
    right, left, mate = ring.dev(1, 0), ring.dev(-1, 0), ring.dev(0, 1)
    started = []

    def part(slot, half):
        return buf.at[pl.ds(slot * CHUNK + 2 * half, 2)]

    def go(index, src, dst, device):
        copy = remote(src, dst, send, recv, index, device)
        copy.start()
        started.append(copy)

    def come(index, ref):
        remote(ref, ref, send, recv, index, right).wait_recv()

    def add(slot, half, ref):
        view = part(slot, half)
        for b in range(2):
            view[b] = (view[b].astype(F32) + ref[b].astype(F32)).astype(BF)

    for dj in (1, 0):
        ready(2, dj)
        slot = ring.at(2, dj)
        go(0 + dj, part(slot, 0), relay_l.at[dj], right)
        go(2 + dj, part(slot, 1), relay_r.at[dj], left)
        yield
    for dj in (1, 0):
        ready(1, dj)
        go(4 + dj, part(ring.at(1, dj), 1), from_l.at[dj, pl.ds(2, 2)], right)
        yield
        ready(-1, dj)
        go(6 + dj, part(ring.at(-1, dj), 0), from_r.at[dj, pl.ds(0, 2)], left)
        yield
    for dj in (1, 0):
        come(0 + dj, relay_l.at[dj])
        add(ring.at(1, dj), 0, relay_l.at[dj])
        go(8 + dj, part(ring.at(1, dj), 0), from_l.at[dj, pl.ds(0, 2)], right)
        yield
        come(2 + dj, relay_r.at[dj])
        add(ring.at(-1, dj), 1, relay_r.at[dj])
        go(10 + dj, part(ring.at(-1, dj), 1), from_r.at[dj, pl.ds(2, 2)], left)
        yield
    ready(0, 1)
    ready(0, 0)
    yield
    for dj in (1, 0):
        slot = ring.at(0, dj)
        for half in range(2):
            piece = pl.ds(2 * half, 2)
            come((8 if half == 0 else 4) + dj, from_l.at[dj, piece])
            come((6 if half == 0 else 10) + dj, from_r.at[dj, piece])
            view = part(slot, half)
            for b in range(2):
                total = (
                    view[b].astype(F32)
                    + from_l[dj, 2 * half + b].astype(F32)
                    + from_r[dj, 2 * half + b].astype(F32)
                )
                if dj == 1:
                    view[b] = total.astype(BF)
                else:
                    finish(2 * half + b, total, None)
            if dj == 1:
                go(12 + half, part(slot, half), from_mate.at[piece], mate)
            yield
    for half in range(2):
        piece = pl.ds(2 * half, 2)
        come(12 + half, from_mate.at[piece])
        for b in range(2):
            finish(2 * half + b, None, from_mate[2 * half + b].astype(F32))
        yield
    for copy in started:
        copy.wait_send()


def drain(steps, times=None):
    if times is None:
        for _ in steps:
            pass
        return
    for _ in range(times):
        next(steps, None)


def fused_kernel(
    n_row, n_col, scale,
    blk_f, src_f, keep_f, end_f, has_f, blk_b, src_b, keep_b, end_b, has_b,
    features, weight, cotangent, values,
    out_ref, gw_ref, gf_ref,
    vbuf, panel, slab, stage, acc, aggbuf, gfbuf, sib_in,
    relay_l, relay_r, from_l, from_r, from_mate,
    crelay_l, crelay_r, cfrom_l, cfrom_r, cfrom_mate,
    agg32, gf32, wterm, wsum, w1, w2,
    local_sem, agc_s, agc_r, agr_s, agr_r, sib_s, sib_r, rsc_s, rsc_r, rsr_s, rsr_r, sx_s, sx_r,
    ws1_s, ws1_r, ws2_s, ws2_r, ws3_s, ws3_r,
):
    row = lax.axis_index("row")
    col = lax.axis_index("col")
    core, yl, x = row % 2, (row // 2) % 2, row // 4
    z, yh = col % 4, col // 4
    sibling = {"row": x * 4 + yl * 2 + (1 - core), "col": col}

    load_values = pltpu.make_async_copy(values, vbuf.at[pl.ds(0, NNZ)], local_sem.at[0])
    load_values.start()
    load_own = pltpu.make_async_copy(features, panel.at[pl.ds(col * CHUNK, CHUNK)], local_sem.at[1])
    load_own.start()

    barrier = pltpu.get_barrier_semaphore()

    @pl.loop(1, n_row)
    def _(d):
        pl.semaphore_signal(barrier, inc=1, device_id={"row": (row + d) % n_row, "col": col}, device_id_type=MESH)

    @pl.loop(1, n_col)
    def _(d):
        pl.semaphore_signal(barrier, inc=1, device_id={"row": row, "col": (col + d) % n_col}, device_id_type=MESH)

    vbuf[NNZ] = jnp.zeros((B, B), BF)
    for b in range(CHUNK):
        slab[row * CHUNK + b] = lax.dot_general(
            cotangent[b], weight[...], (((1,), (1,)), ((), ())), preferred_element_type=F32
        ).astype(BF)
    load_own.wait()
    pl.semaphore_wait(barrier, n_row + n_col - 2)

    ring_c = Ring(z, yh, lambda i, j: j * 4 + i, lambda i, j: {"row": row, "col": j * 4 + i})
    ring_r = Ring(
        x, yl, lambda i, j: i * 4 + j * 2 + core, lambda i, j: {"row": i * 4 + j * 2 + core, "col": col}
    )

    sib_started = []

    def to_sibling(slot, half):
        index = len(sib_started)
        ref = slab.at[pl.ds(slot * CHUNK + 2 * half, 2)]
        copy = remote(ref, ref, sib_s, sib_r, index, sibling)
        copy.start()
        sib_started.append((slot, half, copy))

    ag_c = gather_steps(panel, ring_c, agc_s, agc_r, lambda slot, half: None)
    ag_r = gather_steps(slab, ring_r, agr_s, agr_r, to_sibling)
    done = object()
    next(ag_c)
    next(ag_r)
    for _ in range(12):
        next(ag_c, done)
        next(ag_r, done)
    drain(ag_c)
    drain(ag_r)
    load_values.wait()
    for slot, half, copy in sib_started:
        theirs = slot + 1 - 2 * core
        ref = slab.at[pl.ds(theirs * CHUNK + 2 * half, 2)]
        index = [k for k, item in enumerate(sib_started) if item[2] is copy][0]
        remote(ref, ref, sib_s, sib_r, index, sibling).wait_recv()
        copy.wait_send()

    acc[...] = jnp.zeros_like(acc)

    def forward(t, _):
        a, b = blk_f[0, 2 * t], blk_f[0, 2 * t + 1]
        ca, cb = src_f[0, 2 * t], src_f[0, 2 * t + 1]
        keep = keep_f[0, t].astype(F32)
        left = jnp.concatenate([vbuf[a], vbuf[b]], axis=1)
        rhs = jnp.concatenate([panel[ca], panel[cb]], axis=0)
        total = acc[...] * keep + jnp.dot(left, rhs, preferred_element_type=F32)
        acc[...] = total
        stage[t] = total.astype(BF)
        return 0

    def backward(t, _):
        a, b = blk_b[0, 2 * t], blk_b[0, 2 * t + 1]
        ra, rb = src_b[0, 2 * t], src_b[0, 2 * t + 1]
        keep = keep_b[0, t].astype(F32)
        left = jnp.concatenate([vbuf[a], vbuf[b]], axis=0)
        rhs = jnp.concatenate([slab[ra], slab[rb]], axis=0)
        total = acc[...] * keep + lax.dot_general(
            left, rhs, (((0,), (0,)), ((), ())), preferred_element_type=F32
        )
        acc[...] = total
        stage[t] = total.astype(BF)
        return 0

    lax.fori_loop(0, F_PAIRS, forward, 0)

    def pick(target, slot, end, has):
        for b in range(CHUNK):
            r = slot * CHUNK + b
            target[r] = stage[end[0, r]] * has[0, r].astype(F32).astype(BF)

    order = [(2, 1), (2, 0), (1, 1), (-1, 1), (1, 0), (-1, 0), (0, 1), (0, 0)]
    swaps = []
    for m, (di, dj) in enumerate(order):
        slot = ring_r.at(di, dj) + 1 - 2 * core
        pick(aggbuf, slot, end_f, has_f)
        copy = remote(aggbuf.at[pl.ds(slot * CHUNK, CHUNK)], sib_in.at[pl.ds(m * CHUNK, CHUNK)], sx_s, sx_r, m, sibling)
        copy.start()
        swaps.append(copy)
    for di, dj in order:
        pick(aggbuf, ring_r.at(di, dj), end_f, has_f)

    def ready_r(di, dj):
        m = order.index((di, dj))
        slot = ring_r.at(di, dj)
        ref = sib_in.at[pl.ds(m * CHUNK, CHUNK)]
        remote(ref, ref, sx_s, sx_r, m, sibling).wait_recv()
        for b in range(CHUNK):
            r = slot * CHUNK + b
            aggbuf[r] = (aggbuf[r].astype(F32) + sib_in[m * CHUNK + b].astype(F32)).astype(BF)

    def finish_r(b, total, more):
        if more is None:
            agg32[b] = total
        else:
            agg32[b] = agg32[b] + more

    def finish_c(b, total, more):
        if more is None:
            gf32[b] = total
        else:
            gf_ref[b] = (gf32[b] + more).astype(BF)

    rs_r = scatter_steps(
        aggbuf, ring_r, rsr_s, rsr_r, relay_l, relay_r, from_l, from_r, from_mate, ready_r, finish_r
    )
    acc[...] = jnp.zeros_like(acc)
    cut = B_PAIRS // 8
    for piece in range(8):
        drain(rs_r, 1)
        lax.fori_loop(piece * cut, (piece + 1) * cut, backward, 0)
    rs_c = scatter_steps(
        gfbuf, ring_c, rsc_s, rsc_r, crelay_l, crelay_r, cfrom_l, cfrom_r, cfrom_mate,
        lambda di, dj: pick(gfbuf, ring_c.at(di, dj), end_b, has_b), finish_c,
    )
    for _ in range(6):
        drain(rs_c, 1)
        drain(rs_r, 1)
    drain(rs_c, 2)
    drain(rs_r)
    for copy in swaps:
        copy.wait_send()
    for b in range(CHUNK):
        aggregate = agg32[b].astype(BF)
        out_ref[b] = jnp.dot(aggregate, weight[...], preferred_element_type=F32).astype(BF)
        term = lax.dot_general(
            aggregate, cotangent[b], (((0,), (0,)), ((), ())), preferred_element_type=F32
        )
        if b == 0:
            wterm[...] = term.reshape(wterm.shape)
        else:
            wterm[...] = wterm[...] + term.reshape(wterm.shape)

    def w1_copy(d):
        target = (row + d) % n_row
        return remote(wterm.at[target], w1.at[d - 1], ws1_s, ws1_r, d - 1, {"row": target, "col": col})

    def w2_copy(d):
        target = (col + d) % n_col
        return remote(w2.at[col], w2.at[col], ws2_s, ws2_r, d - 1, {"row": row, "col": target})

    def w3_copy(d):
        target = (row + d) % n_row
        return remote(wsum.at[row], wsum.at[row], ws3_s, ws3_r, d - 1, {"row": target, "col": col})

    @pl.loop(1, n_row)
    def _(d):
        w1_copy(d).start()

    drain(rs_c, 4)
    share = wterm[row]
    for d in range(1, n_row):
        remote(w1.at[d - 1], w1.at[d - 1], ws1_s, ws1_r, d - 1, sibling).wait_recv()
        share = share + w1[d - 1]
    w2[col] = share

    @pl.loop(1, n_col)
    def _(d):
        w2_copy(d).start()

    drain(rs_c, 4)

    @pl.loop(1, n_col)
    def _(d):
        origin = (col + n_col - d) % n_col
        remote(w2.at[origin], w2.at[origin], ws2_s, ws2_r, d - 1, sibling).wait_recv()

    whole = w2[0]
    for c in range(1, n_col):
        whole = whole + w2[c]
    wsum[row] = whole * scale

    @pl.loop(1, n_row)
    def _(d):
        w3_copy(d).start()

    drain(rs_c)

    @pl.loop(1, n_row)
    def _(d):
        origin = (row + n_row - d) % n_row
        remote(wsum.at[origin], wsum.at[origin], ws3_s, ws3_r, d - 1, sibling).wait_recv()

    gw_ref[...] = wsum[...]

    @pl.loop(1, n_row)
    def _(d):
        w1_copy(d).wait_send()
        w3_copy(d).wait_send()

    @pl.loop(1, n_col)
    def _(d):
        w2_copy(d).wait_send()


def body(features, weight, cotangent, block_rows, block_cols, counts, values):
    n_row = lax.axis_size("row")
    n_col = lax.axis_size("col")
    width = features.shape[-1]
    nodes = features.shape[0] * n_row * n_col
    meta = build_meta(block_rows[0], block_cols[0], counts)
    shard = (CHUNK, B, width)

    def vm(*shape, dtype=BF):
        return pltpu.VMEM(shape, dtype)

    dma = pltpu.SemaphoreType.DMA
    wide = (B, width)
    scratch = [
        vm(NNZ + 1, B, B), vm(CHUNK * n_col, *wide), vm(CHUNK * n_row, *wide), vm(F_PAIRS, *wide),
        vm(*wide, dtype=F32), vm(CHUNK * n_row, *wide), vm(CHUNK * n_col, *wide), vm(CHUNK * n_row // 2, *wide),
        vm(2, 2, *wide), vm(2, 2, *wide), vm(2, CHUNK, *wide), vm(2, CHUNK, *wide), vm(*shard),
        vm(2, 2, *wide), vm(2, 2, *wide), vm(2, CHUNK, *wide), vm(2, CHUNK, *wide), vm(*shard),
        vm(*shard, dtype=F32), vm(*shard, dtype=F32),
        vm(n_row, width // n_row, width, dtype=F32), vm(n_row, width // n_row, width, dtype=F32),
        vm(n_row - 1, width // n_row, width, dtype=F32), vm(n_col, width // n_row, width, dtype=F32),
        dma((2,)), dma((14,)), dma((14,)), dma((14,)), dma((14,)), dma((16,)), dma((16,)),
        dma((14,)), dma((14,)), dma((14,)), dma((14,)), dma((8,)), dma((8,)),
        dma((n_row - 1,)), dma((n_row - 1,)), dma((n_col - 1,)), dma((n_col - 1,)), dma((n_row - 1,)), dma((n_row - 1,)),
    ]
    vmem = pl.BlockSpec(memory_space=pltpu.VMEM)
    out, gw, gf = pl.pallas_call(
        functools.partial(fused_kernel, n_row, n_col, float(nodes) ** -0.5),
        out_shape=[
            jax.ShapeDtypeStruct(shard, BF),
            jax.ShapeDtypeStruct((n_row, width // n_row, width), F32),
            jax.ShapeDtypeStruct(shard, BF),
        ],
        in_specs=[pl.BlockSpec(memory_space=pltpu.SMEM)] * 10
        + [pl.BlockSpec(memory_space=pl.ANY), vmem, vmem, pl.BlockSpec(memory_space=pl.ANY)],
        out_specs=[vmem] * 3,
        scratch_shapes=scratch,
        compiler_params=pltpu.CompilerParams(
            collective_id=0, has_side_effects=True, vmem_limit_bytes=60 * 1024 * 1024
        ),
    )(*meta, features.reshape(shard), weight, cotangent.reshape(shard), values[0, 0])
    return out.reshape(features.shape), gw.reshape(width, width), gf.reshape(features.shape)


def solution(mesh):
    placed = (
        P(("row", "col"), None),
        P(),
        P(("col", "row"), None),
        P("row", "col", None),
        P("row", "col", None),
        P("row", "col"),
        P("row", "col", None, None, None),
    )
    return jax.shard_map(
        body,
        mesh=mesh,
        in_specs=placed,
        out_specs=(P(("col", "row"), None), P(), P(("row", "col"), None)),
        check_vma=False,
    )
```

time: 686 us -> 156 us (0.23); the launches traced: 675 us -> 156 us
  matrix products: 348 us -> 0 us
  waiting for transfers between devices: 279 us -> 0 us
  Pallas kernels: 0 us -> 150 us
  local copies, waits for them, and re-layouts: 19.8 us -> 5.01 us
  other arithmetic: 13.5 us -> 0 us
  between operations: 14 us -> 1.29 us
    dot_general x39 -> x0, matrix products: 348 us -> none  [the longest x12 195 us: advance(): jnp.einsum('ko,kif->oif', place_table, product, precision=lax.Precision.H...]
    pallas_call x0 -> x2, Pallas kernels: none -> 150 us  [the longest x1 148 us: body(): pl.pallas_call(functools.partial(fused_kernel, n_row, n_col, float(nodes)...]
    psum x1 -> x0, waiting for transfers between devices: 144 us -> none  [body(): weight_total = lax.psum(weight_term, ('row', 'col'))]
    reduce_scatter x2 -> x0, waiting for transfers between devices: 94.9 us -> none  [the longest x1 94.9 us: body(): lax.psum_scatter(partial_sums, 'row', scatter_dimension=0, tiled=True)]
    all_gather x2 -> x0, waiting for transfers between devices: 39 us -> none  [the longest x1 39 us: body(): grad_slab = lax.all_gather(grad_local, 'row', axis=0, tiled=True)]
    while x2 -> x0, local copies, waits for them, and re-layouts: 18 us -> none  [block_product(): total = lax.fori_loop(0, tile_values.shape[0] // GROUP, advance, total)]
    and x12 -> x0, other arithmetic: 8.68 us -> none  [advance(): active = active & (target >= 0) & (target < out_count)]
  transfers between devices with their start and end apart: 5 -> 0, of which waited for: 3 -> 0; matrix products, arithmetic and copies ran while one was open for 56% -> 0% of each run, Pallas kernels for 0% -> 0%
where the time goes in v1:
time: 156 us
  Pallas kernels  150 us (96%)
  local copies, waits for them, and re-layouts  5.01 us (3%)
    pallas_call x1, Pallas kernels, body(): pl.pallas_call(functools.partial(fused_kernel, n_row, n_col, float(nodes)...  148 us
    unnamed x3, local copies, waits for them, and re-layouts  5.01 us

profile of v1, /device:TPU:1, one launch (start us, length us, event | category | flops | bytes accessed | tf_op | source)
XLA Modules:
  0.0 156.0 jit_solution(5239250549754705277)
XLA Ops:
  1.3 2.1 %shard_map.94 = (s32[1,512]{1,0:T(1,128)}, s32[1,512]{1,0:T(1,128)}, s32[1,256]{1,0:T(1,128)}, s32[1,128]{1,0:T(1,128)}, s32[1,128]{1,0:T(1,128)}, /*index=5*/s3...) custom-call(s32[1,384]{1,0:T(1,128)} %bitcast.14, s32[1,384]{1,0:T(1,128)} %bitcast.15, ...), custom_call_target="tpu_custom_call" | custom-call | tf_op jit(solution)/shard_map/pallas_call | solution.py:76
  3.4 147.6 %shard_map.95 = (bf16[4,128,256]{2,1,0:T(8,128)(2,1)}, f32[16,16,256]{2,1,0:T(8,128)}, bf16[4,128,256]{2,1,0:T(8,128)(2,1)}) custom-call(s32[1,512]{1,0:T(1,128)} %get-tuple-element.16.blk_f, s32[1,512]{1,0:T(1,128)} %get-tuple-element.17.src_f, s32[1,256]{1,0:T(1,128)} %get-tuple-element.18.keep_f, s32[1,128]{1,0:T(1,128)} %get-tuple-element.19.end_f, ...), custom_call_target="tpu_custom_call" | custom-call | tf_op jit(solution)/shard_map/pallas_call | solution.py:510
  151.0 1.7 %copy.14 = bf16[512,256]{1,0:T(8,128)(2,1)} copy(bf16[512,256]{1,0:T(8,128)(2,1)} %bitcast.13) | data formatting | bytes 524288
  152.7 1.7 %copy.15 = f32[256,256]{1,0:T(8,128)} copy(f32[256,256]{1,0:T(8,128)} %bitcast.12) | data formatting | bytes 524288
  154.3 1.7 %copy.16 = bf16[512,256]{1,0:T(8,128)(2,1)} copy(bf16[512,256]{1,0:T(8,128)(2,1)} %bitcast.11) | data formatting | bytes 524288

commit v2 on v1

v2 whole, which is shorter than its diff:
```python
import functools

import jax
import jax.numpy as jnp
from jax import lax
from jax.experimental import pallas as pl
from jax.experimental.pallas import tpu as pltpu
from jax.sharding import PartitionSpec as P

MESH = pl.DeviceIdType.MESH
BF = jnp.bfloat16
F32 = jnp.float32
B = 128
NNZ = 384
SLOTS = 512
F_PAIRS = 224
B_PAIRS = 208
CHUNK = 4
UNROLL = 16
BLK, SRC, KEEP, END, HAS, META = 0, 512, 1024, 1280, 1408, 1536


def meta_kernel(rows_ref, cols_ref, count_ref, meta):
    count = count_ref[0, 0]
    lane_k = lax.broadcasted_iota(jnp.int32, (1, NNZ), 1)
    valid = lane_k < count
    rows = jnp.where(valid, rows_ref[...], 900).astype(F32)
    cols = jnp.where(valid, cols_ref[...], 900).astype(F32)
    rows_t = jnp.transpose(jnp.broadcast_to(rows, (B, NNZ)))
    cols_t = jnp.transpose(jnp.broadcast_to(cols, (B, NNZ)))
    sub_k = lax.broadcasted_iota(jnp.int32, (NNZ, B), 0).astype(F32)
    lane_r = lax.broadcasted_iota(jnp.int32, (NNZ, B), 1).astype(F32)
    sub_kk = lax.broadcasted_iota(jnp.int32, (NNZ, NNZ), 0)
    lane_kk = lax.broadcasted_iota(jnp.int32, (NNZ, NNZ), 1)
    sub_r = lax.broadcasted_iota(jnp.int32, (B, NNZ), 0).astype(F32)
    sub_q = lax.broadcasted_iota(jnp.int32, (B, B), 0)
    lane_q = lax.broadcasted_iota(jnp.int32, (B, B), 1)

    def half_up(n):
        return ((n.astype(jnp.int32) + 1) >> 1).astype(F32)

    def one(key, key_t, src_t, base):
        key_tt = jnp.concatenate([key_t] * (NNZ // B), axis=1)
        same = (key_tt == jnp.broadcast_to(key, (NNZ, NNZ))) & (sub_kk < lane_kk)
        within = jnp.sum(jnp.where(same, 1.0, 0.0), axis=0, keepdims=True)
        n_l = jnp.sum(jnp.where(key_t == lane_r, 1.0, 0.0), axis=0, keepdims=True)
        hot = jnp.where(sub_r == jnp.broadcast_to(key, (B, NNZ)), 1.0, 0.0)
        n_s = jnp.sum(hot, axis=1, keepdims=True)
        q_l = half_up(n_l)
        q_s = half_up(n_s)
        s_l = jnp.sum(jnp.where(sub_q < lane_q, jnp.broadcast_to(q_s, (B, B)), 0.0), axis=0, keepdims=True)
        s_s = jnp.sum(jnp.where(lane_q < sub_q, jnp.broadcast_to(q_l, (B, B)), 0.0), axis=1, keepdims=True)
        slot = 2.0 * jnp.sum(hot * s_s, axis=0, keepdims=True) + within
        slot = jnp.where(valid, slot, 9000.0)
        slot_t = jnp.transpose(jnp.broadcast_to(slot, (B, NNZ)))
        src_clean = jnp.where(src_t < 800.0, src_t, 0.0)
        for part in range(SLOTS // B):
            match = slot_t == lane_r + float(part * B)
            found = jnp.sum(jnp.where(match, sub_k + 1.0, 0.0), axis=0, keepdims=True)
            where = jnp.sum(jnp.where(match, src_clean, 0.0), axis=0, keepdims=True)
            found = jnp.where(found == 0.0, float(NNZ + 1), found) - 1.0
            meta[:, pl.ds(base + BLK + part * B, B)] = found.astype(jnp.int32)
            meta[:, pl.ds(base + SRC + part * B, B)] = where.astype(jnp.int32)
        for part in range(2):
            first = (s_s == (lane_q + part * B).astype(F32)) & (n_s > 0.0)
            starts = jnp.sum(jnp.where(first, 1.0, 0.0), axis=0, keepdims=True)
            meta[:, pl.ds(base + KEEP + part * B, B)] = (1.0 - starts).astype(jnp.int32)
        ends = jnp.where(n_l > 0.0, s_l + q_l - 1.0, 0.0)
        meta[:, pl.ds(base + END, B)] = ends.astype(jnp.int32)
        meta[:, pl.ds(base + HAS, B)] = jnp.where(n_l > 0.0, 1.0, 0.0).astype(jnp.int32)

    one(rows, rows_t, cols_t, 0)
    one(cols, cols_t, rows_t, META)


def build_meta(block_rows, block_cols, counts):
    return pl.pallas_call(
        meta_kernel,
        out_shape=jax.ShapeDtypeStruct((1, 2 * META), jnp.int32),
        in_specs=[
            pl.BlockSpec(memory_space=pltpu.VMEM),
            pl.BlockSpec(memory_space=pltpu.VMEM),
            pl.BlockSpec(memory_space=pltpu.SMEM),
        ],
        out_specs=pl.BlockSpec(memory_space=pltpu.VMEM),
    )(block_rows, block_cols, counts)


def hand_over(src_a, src_b, src_c, dst_a, dst_b, dst_c):
    dst_a[...] = src_a[...]
    dst_b[...] = src_b[...]
    dst_c[...] = src_c[...]


class Ring:
    def __init__(self, i, j, slot, device):
        self.i, self.j, self.slot, self.device = i, j, slot, device

    def at(self, di, dj):
        i = (self.i + di + 4) % 4
        j = self.j if dj == 0 else 1 - self.j
        return self.slot(i, j)

    def dev(self, di, dj):
        i = (self.i + di + 4) % 4
        j = self.j if dj == 0 else 1 - self.j
        return self.device(i, j)


def remote(src, dst, send, recv, index, device):
    return pltpu.make_async_remote_copy(
        src_ref=src, dst_ref=dst, send_sem=send.at[index], recv_sem=recv.at[index], device_id=device, device_id_type=MESH
    )


def gather_steps(buf, ring, send, recv, arrived, pair_first):
    def part(slot, half):
        return buf.at[pl.ds(slot * CHUNK + 2 * half, 2)]

    right, left, mate = ring.dev(1, 0), ring.dev(-1, 0), ring.dev(0, 1)
    started = []

    def go(index, slot, half, device):
        copy = remote(part(slot, half), part(slot, half), send, recv, index, device)
        copy.start()
        started.append(copy)

    def come(index, slot, half):
        remote(part(slot, half), part(slot, half), send, recv, index, right).wait_recv()
        arrived(slot, half)

    own, other = ring.at(0, 0), ring.at(0, 1)
    if pair_first:
        go(0, own, 0, mate)
    go(2, own, 0, right)
    go(8, own, 1, left)
    if pair_first:
        go(1, own, 1, mate)
    go(3, own, 1, right)
    go(9, own, 0, left)
    arrived(own, 0)
    arrived(own, 1)
    yield
    come(2, ring.at(-1, 0), 0)
    go(6, ring.at(-1, 0), 0, right)
    if not pair_first:
        go(0, own, 0, mate)
        go(1, own, 1, mate)
    yield
    come(8, ring.at(1, 0), 1)
    go(12, ring.at(1, 0), 1, left)
    yield
    come(0, other, 0)
    go(4, other, 0, right)
    go(11, other, 0, left)
    yield
    come(1, other, 1)
    go(10, other, 1, left)
    go(5, other, 1, right)
    yield
    come(3, ring.at(-1, 0), 1)
    come(9, ring.at(1, 0), 0)
    yield
    come(4, ring.at(-1, 1), 0)
    go(7, ring.at(-1, 1), 0, right)
    yield
    come(10, ring.at(1, 1), 1)
    go(13, ring.at(1, 1), 1, left)
    yield
    come(6, ring.at(-2, 0), 0)
    come(12, ring.at(2, 0), 1)
    yield
    come(5, ring.at(-1, 1), 1)
    come(11, ring.at(1, 1), 0)
    yield
    come(7, ring.at(-2, 1), 0)
    come(13, ring.at(2, 1), 1)
    for copy in started:
        copy.wait_send()


def scatter_steps(buf, ring, send, recv, relay_l, relay_r, from_l, from_r, from_mate, ready, after, finish):
    right, left, mate = ring.dev(1, 0), ring.dev(-1, 0), ring.dev(0, 1)
    started = []

    def part(slot, half):
        return buf.at[pl.ds(slot * CHUNK + 2 * half, 2)]

    def go(index, src, dst, device):
        copy = remote(src, dst, send, recv, index, device)
        copy.start()
        started.append(copy)

    def come(index, ref):
        remote(ref, ref, send, recv, index, right).wait_recv()

    def add(slot, half, ref):
        view = part(slot, half)
        for b in range(2):
            view[b] = (view[b].astype(F32) + ref[b].astype(F32)).astype(BF)

    def feed(dj):
        ready(2, dj)
        slot = ring.at(2, dj)
        go(0 + dj, part(slot, 0), relay_l.at[dj], right)
        go(2 + dj, part(slot, 1), relay_r.at[dj], left)
        after(2, dj)
        yield
        ready(1, dj)
        go(4 + dj, part(ring.at(1, dj), 1), from_l.at[dj, pl.ds(2, 2)], right)
        after(1, dj)
        yield
        ready(-1, dj)
        go(6 + dj, part(ring.at(-1, dj), 0), from_r.at[dj, pl.ds(0, 2)], left)
        after(-1, dj)
        yield

    def relay(dj):
        come(0 + dj, relay_l.at[dj])
        add(ring.at(1, dj), 0, relay_l.at[dj])
        go(8 + dj, part(ring.at(1, dj), 0), from_l.at[dj, pl.ds(0, 2)], right)
        yield
        come(2 + dj, relay_r.at[dj])
        add(ring.at(-1, dj), 1, relay_r.at[dj])
        go(10 + dj, part(ring.at(-1, dj), 1), from_r.at[dj, pl.ds(2, 2)], left)
        yield

    def landed(dj, half):
        piece = pl.ds(2 * half, 2)
        come((8 if half == 0 else 4) + dj, from_l.at[dj, piece])
        come((6 if half == 0 else 10) + dj, from_r.at[dj, piece])

    def total(dj, k):
        r = ring.at(0, dj) * CHUNK + k
        return buf[r].astype(F32) + from_l[dj, k].astype(F32) + from_r[dj, k].astype(F32)

    yield from feed(1)
    yield from relay(1)
    yield from feed(0)
    for dj in (1, 0):
        ready(0, dj)
        after(0, dj)
    yield
    for half in range(2):
        landed(1, half)
        for k in (2 * half, 2 * half + 1):
            buf[ring.at(0, 1) * CHUNK + k] = total(1, k).astype(BF)
        go(12 + half, part(ring.at(0, 1), half), from_mate.at[pl.ds(2 * half, 2)], mate)
    yield
    yield from relay(0)
    for half in range(2):
        landed(0, half)
        come(12 + half, from_mate.at[pl.ds(2 * half, 2)])
        for k in (2 * half, 2 * half + 1):
            finish(k, total(0, k) + from_mate[k].astype(F32))
    for copy in started:
        copy.wait_send()


def drain(steps, times=None):
    if times is None:
        for _ in steps:
            pass
        return
    for _ in range(times):
        next(steps, None)


def fused_kernel(
    n_row, n_col, scale,
    meta, features, weight, cotangent, values,
    out_ref, gw_ref, gf_ref,
    vbuf, panel, cslab, slab, stage, acc, aggbuf, gfbuf, sib_in,
    relay_l, relay_r, from_l, from_r, from_mate,
    crelay_l, crelay_r, cfrom_l, cfrom_r, cfrom_mate,
    agg, wterm, wsum, w1, w2, whalf,
    local_sem, agc_s, agc_r, agr_s, agr_r, sib_s, sib_r, rsc_s, rsc_r, rsr_s, rsr_r, sx_s, sx_r,
    ws1_s, ws1_r, ws2_s, ws2_r, ws3_s, ws3_r, wc_s, wc_r,
):
    row = lax.axis_index("row")
    col = lax.axis_index("col")
    core, yl, x = row % 2, (row // 2) % 2, row // 4
    z, yh = col % 4, col // 4
    sibling = {"row": x * 4 + yl * 2 + (1 - core), "col": col}

    load_values = pltpu.make_async_copy(values, vbuf.at[pl.ds(0, NNZ)], local_sem.at[0])
    load_values.start()
    load_own = pltpu.make_async_copy(features, panel.at[pl.ds(col * CHUNK, CHUNK)], local_sem.at[1])
    load_own.start()
    load_cot = pltpu.make_async_copy(cotangent, cslab.at[pl.ds(row * CHUNK, CHUNK)], local_sem.at[2])
    load_cot.start()

    barrier = pltpu.get_barrier_semaphore()

    @pl.loop(1, n_row)
    def _(d):
        pl.semaphore_signal(barrier, inc=1, device_id={"row": (row + d) % n_row, "col": col}, device_id_type=MESH)

    @pl.loop(1, n_col)
    def _(d):
        pl.semaphore_signal(barrier, inc=1, device_id={"row": row, "col": (col + d) % n_col}, device_id_type=MESH)

    vbuf[NNZ] = jnp.zeros((B, B), BF)
    load_own.wait()
    load_cot.wait()
    pl.semaphore_wait(barrier, n_row + n_col - 2)

    ring_c = Ring(z, yh, lambda i, j: j * 4 + i, lambda i, j: {"row": row, "col": j * 4 + i})
    ring_r = Ring(
        x, yl, lambda i, j: i * 4 + j * 2 + core, lambda i, j: {"row": i * 4 + j * 2 + core, "col": col}
    )

    sib_started = []
    sib_taken = []

    def backprop(slot, half):
        piece = pl.ds(slot * CHUNK + 2 * half, 2)
        rows = cslab[piece].reshape(2 * B, cslab.shape[-1])
        grad = lax.dot_general(rows, weight[...], (((1,), (1,)), ((), ())), preferred_element_type=F32)
        slab[piece] = grad.astype(BF).reshape(2, B, cslab.shape[-1])

    def from_sibling(upto):
        while len(sib_taken) < upto:
            index = len(sib_taken)
            slot, half, copy = sib_started[index]
            theirs = slot + 1 - 2 * core
            ref = cslab.at[pl.ds(theirs * CHUNK + 2 * half, 2)]
            remote(ref, ref, sib_s, sib_r, index, sibling).wait_recv()
            backprop(theirs, half)
            sib_taken.append(copy)

    def to_sibling(slot, half):
        index = len(sib_started)
        ref = cslab.at[pl.ds(slot * CHUNK + 2 * half, 2)]
        copy = remote(ref, ref, sib_s, sib_r, index, sibling)
        copy.start()
        backprop(slot, half)
        from_sibling(index - 2)
        sib_started.append((slot, half, copy))

    ag_c = gather_steps(panel, ring_c, agc_s, agc_r, lambda slot, half: None, True)
    ag_r = gather_steps(cslab, ring_r, agr_s, agr_r, to_sibling, False)
    done = object()
    next(ag_c)
    next(ag_r)
    for index in range(9):
        next(ag_c, done)
        if index >= 1:
            next(ag_r, done)
    drain(ag_c)
    load_values.wait()
    acc[...] = jnp.zeros_like(acc)
    def forward(t, _):
        a, b = meta[0, BLK + 2 * t], meta[0, BLK + 2 * t + 1]
        ca, cb = meta[0, SRC + 2 * t], meta[0, SRC + 2 * t + 1]
        keep = meta[0, KEEP + t].astype(F32)
        left = jnp.concatenate([vbuf[a], vbuf[b]], axis=1)
        rhs = jnp.concatenate([panel[ca], panel[cb]], axis=0)
        total = acc[...] * keep + jnp.dot(left, rhs, preferred_element_type=F32)
        acc[...] = total
        stage[t] = total.astype(BF)
        return 0

    def backward(t, _):
        a, b = meta[0, META + BLK + 2 * t], meta[0, META + BLK + 2 * t + 1]
        ra, rb = meta[0, META + SRC + 2 * t], meta[0, META + SRC + 2 * t + 1]
        keep = meta[0, META + KEEP + t].astype(F32)
        left = jnp.concatenate([vbuf[a], vbuf[b]], axis=0)
        rhs = jnp.concatenate([slab[ra], slab[rb]], axis=0)
        total = acc[...] * keep + lax.dot_general(
            left, rhs, (((0,), (0,)), ((), ())), preferred_element_type=F32
        )
        acc[...] = total
        stage[t] = total.astype(BF)
        return 0

    f_cut = F_PAIRS // 7
    for piece in range(7):
        lax.fori_loop(piece * f_cut, (piece + 1) * f_cut, forward, 0, unroll=UNROLL)
        next(ag_r, done)
    drain(ag_r)

    def pick(target, slot, base):
        for b in range(CHUNK):
            r = slot * CHUNK + b
            target[r] = stage[meta[0, base + END + r]] * meta[0, base + HAS + r].astype(F32).astype(BF)

    order = [(2, 1), (1, 1), (-1, 1), (2, 0), (1, 0), (-1, 0), (0, 1), (0, 0)]
    swaps = []
    for m, (di, dj) in enumerate(order):
        slot = ring_r.at(di, dj) + 1 - 2 * core
        pick(aggbuf, slot, 0)
        copy = remote(aggbuf.at[pl.ds(slot * CHUNK, CHUNK)], sib_in.at[pl.ds(m * CHUNK, CHUNK)], sx_s, sx_r, m, sibling)
        copy.start()
        swaps.append(copy)
    for di, dj in order:
        pick(aggbuf, ring_r.at(di, dj), 0)

    def ready_r(di, dj):
        m = order.index((di, dj))
        slot = ring_r.at(di, dj)
        ref = sib_in.at[pl.ds(m * CHUNK, CHUNK)]
        remote(ref, ref, sx_s, sx_r, m, sibling).wait_recv()
        for b in range(CHUNK):
            r = slot * CHUNK + b
            aggbuf[r] = (aggbuf[r].astype(F32) + sib_in[m * CHUNK + b].astype(F32)).astype(BF)

    seen = []

    def after_r(di, dj):
        piece = pl.ds(ring_r.at(di, dj) * CHUNK, CHUNK)
        width = aggbuf.shape[-1]
        term = lax.dot_general(
            aggbuf[piece].reshape(CHUNK * B, width), cslab[piece].reshape(CHUNK * B, width),
            (((0,), (0,)), ((), ())), preferred_element_type=F32,
        ).reshape(wterm.shape)
        wterm[...] = wterm[...] + term if seen else term
        seen.append((di, dj))

    def finish_r(k, total):
        agg[k] = total.astype(BF)

    def finish_c(k, total):
        gf_ref[k] = total.astype(BF)

    rs_r = scatter_steps(
        aggbuf, ring_r, rsr_s, rsr_r, relay_l, relay_r, from_l, from_r, from_mate, ready_r, after_r, finish_r
    )
    acc[...] = jnp.zeros_like(acc)
    from_sibling(16)
    for copy in sib_taken:
        copy.wait_send()
    for piece in range(13):
        lax.fori_loop(piece * UNROLL, (piece + 1) * UNROLL, backward, 0, unroll=UNROLL)
        if piece in (0, 1, 2, 6, 7, 8, 9, 10, 12):
            drain(rs_r, 1)
    rs_c = scatter_steps(
        gfbuf, ring_c, rsc_s, rsc_r, crelay_l, crelay_r, cfrom_l, cfrom_r, cfrom_mate,
        lambda di, dj: pick(gfbuf, ring_c.at(di, dj), META), lambda di, dj: None, finish_c,
    )
    spot = x * 2 + yl
    n_chip = n_row // 2

    def chip(d):
        other = (spot + d) % n_chip
        return other, {"row": other * 2 + core, "col": col}

    def w1_copy(d):
        other, device = chip(d)
        return remote(wterm.at[core, other], w1.at[d - 1], ws1_s, ws1_r, d - 1, device)

    def w2_copy(d):
        target = (col + d) % n_col
        return remote(w2.at[col], w2.at[col], ws2_s, ws2_r, d - 1, {"row": row, "col": target})

    def w3_copy(d):
        _, device = chip(d)
        return remote(wsum.at[core, spot], wsum.at[core, spot], ws3_s, ws3_r, d - 1, device)

    drain(rs_c, 3)
    to_core = remote(wterm.at[1 - core], whalf, wc_s, wc_r, 0, sibling)
    to_core.start()
    drain(rs_r, 1)
    to_core.wait_recv()
    wterm[core] = wterm[core] + whalf[...]
    for d in range(1, n_chip):
        w1_copy(d).start()
    drain(rs_c, 5)
    drain(rs_r, 2)
    share = wterm[core, spot]
    for d in range(1, n_chip):
        w1_copy(d).wait_recv()
        share = share + w1[d - 1]
    w2[col] = share
    for d in range(1, n_col):
        w2_copy(d).start()
    drain(rs_c, 2)
    drain(rs_r)
    for copy in swaps:
        copy.wait_send()
    for b in range(CHUNK):
        out_ref[b] = jnp.dot(agg[b], weight[...], preferred_element_type=F32).astype(BF)
    for d in range(1, n_col):
        origin = (col + n_col - d) % n_col
        remote(w2.at[origin], w2.at[origin], ws2_s, ws2_r, d - 1, sibling).wait_recv()
    whole = w2[0]
    for c in range(1, n_col):
        whole = whole + w2[c]
    wsum[core, spot] = whole * scale
    for d in range(1, n_chip):
        w3_copy(d).start()
    drain(rs_c, 2)
    for d in range(1, n_chip):
        origin = (spot + n_chip - d) % n_chip
        remote(wsum.at[core, origin], wsum.at[core, origin], ws3_s, ws3_r, d - 1, sibling).wait_recv()
    back = remote(wsum.at[core], wsum.at[core], wc_s, wc_r, 1, sibling)
    back.start()
    drain(rs_c)
    remote(wsum.at[1 - core], wsum.at[1 - core], wc_s, wc_r, 1, sibling).wait_recv()
    gw_ref[...] = wsum[...]
    for d in range(1, n_chip):
        w1_copy(d).wait_send()
        w3_copy(d).wait_send()
    for d in range(1, n_col):
        w2_copy(d).wait_send()
    to_core.wait_send()
    back.wait_send()


def body(features, weight, cotangent, block_rows, block_cols, counts, values):
    n_row = lax.axis_size("row")
    n_col = lax.axis_size("col")
    width = features.shape[-1]
    nodes = features.shape[0] * n_row * n_col
    meta = build_meta(block_rows[0], block_cols[0], counts)
    shard = (CHUNK, B, width)

    def vm(*shape, dtype=BF):
        return pltpu.VMEM(shape, dtype)

    dma = pltpu.SemaphoreType.DMA
    wide = (B, width)
    scratch = [
        vm(NNZ + 1, B, B), vm(CHUNK * n_col, *wide), vm(CHUNK * n_row, *wide), vm(CHUNK * n_row, *wide), vm(F_PAIRS, *wide),
        vm(*wide, dtype=F32), vm(CHUNK * n_row, *wide), vm(CHUNK * n_col, *wide), vm(CHUNK * n_row // 2, *wide),
        vm(2, 2, *wide), vm(2, 2, *wide), vm(2, CHUNK, *wide), vm(2, CHUNK, *wide), vm(*shard),
        vm(2, 2, *wide), vm(2, 2, *wide), vm(2, CHUNK, *wide), vm(2, CHUNK, *wide), vm(*shard),
        vm(*shard),
        vm(2, n_row // 2, width // n_row, width, dtype=F32), vm(2, n_row // 2, width // n_row, width, dtype=F32),
        vm(n_row // 2 - 1, width // n_row, width, dtype=F32), vm(n_col, width // n_row, width, dtype=F32),
        vm(n_row // 2, width // n_row, width, dtype=F32),
        dma((3,)), dma((14,)), dma((14,)), dma((14,)), dma((14,)), dma((16,)), dma((16,)),
        dma((14,)), dma((14,)), dma((14,)), dma((14,)), dma((8,)), dma((8,)),
        dma((n_row // 2 - 1,)), dma((n_row // 2 - 1,)), dma((n_col - 1,)), dma((n_col - 1,)),
        dma((n_row // 2 - 1,)), dma((n_row // 2 - 1,)), dma((2,)), dma((2,)),
    ]
    vmem = pl.BlockSpec(memory_space=pltpu.VMEM)
    out, gw, gf = pl.pallas_call(
        functools.partial(fused_kernel, n_row, n_col, float(nodes) ** -0.5),
        out_shape=[
            jax.ShapeDtypeStruct(shard, BF),
            jax.ShapeDtypeStruct((2, n_row // 2, width // n_row, width), F32),
            jax.ShapeDtypeStruct(shard, BF),
        ],
        in_specs=[pl.BlockSpec(memory_space=pltpu.SMEM), pl.BlockSpec(memory_space=pl.ANY), vmem] + [pl.BlockSpec(memory_space=pl.ANY)] * 2,
        out_specs=[vmem] * 3,
        scratch_shapes=scratch,
        compiler_params=pltpu.CompilerParams(
            collective_id=0, has_side_effects=True, vmem_limit_bytes=60 * 1024 * 1024
        ),
    )(meta, features.reshape(shard), weight, cotangent.reshape(shard), values[0, 0])
    out, gw, gf = pl.pallas_call(
        hand_over,
        out_shape=[jax.ShapeDtypeStruct(item.shape, item.dtype) for item in (out, gw, gf)],
        in_specs=[vmem] * 3,
        out_specs=[vmem] * 3,
    )(out, gw, gf)
    return out.reshape(features.shape), gw.reshape(width, width), gf.reshape(features.shape)


def solution(mesh):
    placed = (
        P(("row", "col"), None),
        P(),
        P(("col", "row"), None),
        P("row", "col", None),
        P("row", "col", None),
        P("row", "col"),
        P("row", "col", None, None, None),
    )
    return jax.shard_map(
        body,
        mesh=mesh,
        in_specs=placed,
        out_specs=(P(("col", "row"), None), P(), P(("row", "col"), None)),
        check_vma=False,
    )
```

time: 156 us -> 82.3 us (0.53)
  Pallas kernels: 150 us -> 80.8 us
  local copies, waits for them, and re-layouts: 5.01 us -> 0 us
    pallas_call x1, Pallas kernels: 148 us -> 76.7 us  [body(): pl.pallas_call(functools.partial(fused_kernel, n_row, n_col, float(nodes)...]
    unnamed x3 -> x0, local copies, waits for them, and re-layouts: 5.01 us -> none
    pallas_call x1 -> x2, Pallas kernels: 2.09 us -> 4.1 us  [the longest x1 2.09 us: build_meta(): pl.pallas_call(meta_kernel, out_shape=jax.ShapeDtypeStruct((1, 2 * META),...]
where the time goes in v2:
time: 82.3 us; the launch traced here: 82.1 us
  Pallas kernels  80.8 us (98%)
  between operations  1.29 us (2%)
    pallas_call x1, Pallas kernels, body(): pl.pallas_call(functools.partial(fused_kernel, n_row, n_col, float(nodes)...  76.7 us
    pallas_call x1, Pallas kernels, build_meta(): pl.pallas_call(meta_kernel, out_shape=jax.ShapeDtypeStruct((1, 2 * META),...  2.09 us
    pallas_call x1, Pallas kernels, body(): pl.pallas_call(hand_over, out_shape=[jax.ShapeDtypeStruct(item.shape, ite...  2 us

profile of v2, /device:TPU:1, one launch (start us, length us, event | category | flops | bytes accessed | tf_op | source)
XLA Modules:
  0.0 82.1 jit_solution(17444331168815310539)
XLA Ops:
  1.3 2.1 %shard_map.94.meta = s32[1,3072]{1,0:T(1,128)} custom-call(s32[1,384]{1,0:T(1,128)} %bitcast.11, s32[1,384]{1,0:T(1,128)} %bitcast.12, s32[1,1]{1,0:T(1,128)S(6)} %copy.10.count_ref), custom_call_target="tpu_custom_call" | custom-call | tf_op jit(solution)/shard_map/pallas_call | solution.py:77
  3.4 76.7 %shard_map.95 = (bf16[4,128,256]{2,1,0:T(8,128)(2,1)}, f32[2,8,16,256]{3,2,1,0:T(8,128)}, bf16[4,128,256]{2,1,0:T(8,128)(2,1)}) custom-call(s32[1,3072]{1,0:T(1,128)} %shard_map.94.meta, bf16[4,128,256]{2,1,0:T(8,128)(2,1)} %bitcast.9, bf16[256,256]{1,0:T(8,128)(2,1)} %weight.1, bf16[4,128,256]{2,1,0:T(8,128)(2,1)} %bitcast.10, bf16[384,128,128]{2,1,0:T(8,128)(2,1)} %bitcast.8), custom_call_target="tpu_custom_call" | custom-call | tf_op jit(solution)/shard_map/pallas_call | solution.py:538
  80.1 2.0 %shard_map.96 = (bf16[4,128,256]{2,1,0:T(8,128)(2,1)}, f32[2,8,16,256]{3,2,1,0:T(8,128)}, bf16[4,128,256]{2,1,0:T(8,128)(2,1)}) custom-call(bf16[4,128,256]{2,1,0:T(8,128)(2,1)} %get-tuple-element.9.src_a, f32[2,8,16,256]{3,2,1,0:T(8,128)} %get-tuple-element.10.src_b, bf16[4,128,256]{2,1,0:T(8,128)(2,1)} %get-tuple-element.11.src_c), custom_call_target="tpu_custom_call" | custom-call | tf_op jit(solution)/shard_map/pallas_call | solution.py:552

commit v3 on v2

--- a/solution.py
+++ b/solution.py
@@ -20,70 +20,55 @@
 BLK, SRC, KEEP, END, HAS, META = 0, 512, 1024, 1280, 1408, 1536
 
 
-def meta_kernel(rows_ref, cols_ref, count_ref, meta):
+def sort_blocks(rows_ref, cols_ref, count_ref, meta):
     count = count_ref[0, 0]
-    lane_k = lax.broadcasted_iota(jnp.int32, (1, NNZ), 1)
-    valid = lane_k < count
-    rows = jnp.where(valid, rows_ref[...], 900).astype(F32)
-    cols = jnp.where(valid, cols_ref[...], 900).astype(F32)
+
+    def iota(shape, axis):
+        return lax.broadcasted_iota(jnp.int32, shape, axis)
+
+    valid = iota((1, NNZ), 1) < count
+    rows = jnp.where(valid, rows_ref[...], 900)
+    cols = jnp.where(valid, cols_ref[...], 900)
     rows_t = jnp.transpose(jnp.broadcast_to(rows, (B, NNZ)))
     cols_t = jnp.transpose(jnp.broadcast_to(cols, (B, NNZ)))
-    sub_k = lax.broadcasted_iota(jnp.int32, (NNZ, B), 0).astype(F32)
-    lane_r = lax.broadcasted_iota(jnp.int32, (NNZ, B), 1).astype(F32)
-    sub_kk = lax.broadcasted_iota(jnp.int32, (NNZ, NNZ), 0)
-    lane_kk = lax.broadcasted_iota(jnp.int32, (NNZ, NNZ), 1)
-    sub_r = lax.broadcasted_iota(jnp.int32, (B, NNZ), 0).astype(F32)
-    sub_q = lax.broadcasted_iota(jnp.int32, (B, B), 0)
-    lane_q = lax.broadcasted_iota(jnp.int32, (B, B), 1)
-
-    def half_up(n):
-        return ((n.astype(jnp.int32) + 1) >> 1).astype(F32)
+    sub_k = iota((NNZ, B), 0)
+    lane_r = iota((NNZ, B), 1)
+    earlier = iota((NNZ, NNZ), 0) < iota((NNZ, NNZ), 1)
+    sub_r = iota((B, NNZ), 0)
+    sub_q = iota((B, B), 0)
+    lane_q = iota((B, B), 1)
+
+    def count_up(mask, axis):
+        return jnp.sum(jnp.where(mask, 1, 0), axis=axis, keepdims=True)
 
     def one(key, key_t, src_t, base):
         key_tt = jnp.concatenate([key_t] * (NNZ // B), axis=1)
-        same = (key_tt == jnp.broadcast_to(key, (NNZ, NNZ))) & (sub_kk < lane_kk)
-        within = jnp.sum(jnp.where(same, 1.0, 0.0), axis=0, keepdims=True)
-        n_l = jnp.sum(jnp.where(key_t == lane_r, 1.0, 0.0), axis=0, keepdims=True)
-        hot = jnp.where(sub_r == jnp.broadcast_to(key, (B, NNZ)), 1.0, 0.0)
-        n_s = jnp.sum(hot, axis=1, keepdims=True)
-        q_l = half_up(n_l)
-        q_s = half_up(n_s)
-        s_l = jnp.sum(jnp.where(sub_q < lane_q, jnp.broadcast_to(q_s, (B, B)), 0.0), axis=0, keepdims=True)
-        s_s = jnp.sum(jnp.where(lane_q < sub_q, jnp.broadcast_to(q_l, (B, B)), 0.0), axis=1, keepdims=True)
-        slot = 2.0 * jnp.sum(hot * s_s, axis=0, keepdims=True) + within
-        slot = jnp.where(valid, slot, 9000.0)
+        within = count_up((key_tt == jnp.broadcast_to(key, (NNZ, NNZ))) & earlier, 0)
+        n_l = count_up(key_t == lane_r, 0)
+        hot = sub_r == jnp.broadcast_to(key, (B, NNZ))
+        n_s = count_up(hot, 1)
+        q_l = (n_l + 1) >> 1
+        q_s = (n_s + 1) >> 1
+        s_l = jnp.sum(jnp.where(sub_q < lane_q, jnp.broadcast_to(q_s, (B, B)), 0), axis=0, keepdims=True)
+        s_s = jnp.sum(jnp.where(lane_q < sub_q, jnp.broadcast_to(q_l, (B, B)), 0), axis=1, keepdims=True)
+        slot = 2 * jnp.sum(jnp.where(hot, jnp.broadcast_to(s_s, (B, NNZ)), 0), axis=0, keepdims=True) + within
+        slot = jnp.where(valid, slot, 9000)
         slot_t = jnp.transpose(jnp.broadcast_to(slot, (B, NNZ)))
-        src_clean = jnp.where(src_t < 800.0, src_t, 0.0)
+        src_clean = jnp.where(src_t < 800, src_t, 0)
         for part in range(SLOTS // B):
-            match = slot_t == lane_r + float(part * B)
-            found = jnp.sum(jnp.where(match, sub_k + 1.0, 0.0), axis=0, keepdims=True)
-            where = jnp.sum(jnp.where(match, src_clean, 0.0), axis=0, keepdims=True)
-            found = jnp.where(found == 0.0, float(NNZ + 1), found) - 1.0
-            meta[:, pl.ds(base + BLK + part * B, B)] = found.astype(jnp.int32)
-            meta[:, pl.ds(base + SRC + part * B, B)] = where.astype(jnp.int32)
+            match = slot_t == lane_r + part * B
+            found = jnp.sum(jnp.where(match, sub_k + 1, 0), axis=0, keepdims=True)
+            where = jnp.sum(jnp.where(match, src_clean, 0), axis=0, keepdims=True)
+            meta[:, pl.ds(base + BLK + part * B, B)] = jnp.where(found == 0, NNZ, found - 1)
+            meta[:, pl.ds(base + SRC + part * B, B)] = where
         for part in range(2):
-            first = (s_s == (lane_q + part * B).astype(F32)) & (n_s > 0.0)
-            starts = jnp.sum(jnp.where(first, 1.0, 0.0), axis=0, keepdims=True)
-            meta[:, pl.ds(base + KEEP + part * B, B)] = (1.0 - starts).astype(jnp.int32)
-        ends = jnp.where(n_l > 0.0, s_l + q_l - 1.0, 0.0)
-        meta[:, pl.ds(base + END, B)] = ends.astype(jnp.int32)
-        meta[:, pl.ds(base + HAS, B)] = jnp.where(n_l > 0.0, 1.0, 0.0).astype(jnp.int32)
+            first = (s_s == lane_q + part * B) & (n_s > 0)
+            meta[:, pl.ds(base + KEEP + part * B, B)] = 1 - count_up(first, 0)
+        meta[:, pl.ds(base + END, B)] = jnp.where(n_l > 0, s_l + q_l - 1, 0)
+        meta[:, pl.ds(base + HAS, B)] = jnp.where(n_l > 0, 1, 0)
 
     one(rows, rows_t, cols_t, 0)
     one(cols, cols_t, rows_t, META)
-
-
-def build_meta(block_rows, block_cols, counts):
-    return pl.pallas_call(
-        meta_kernel,
-        out_shape=jax.ShapeDtypeStruct((1, 2 * META), jnp.int32),
-        in_specs=[
-            pl.BlockSpec(memory_space=pltpu.VMEM),
-            pl.BlockSpec(memory_space=pltpu.VMEM),
-            pl.BlockSpec(memory_space=pltpu.SMEM),
-        ],
-        out_specs=pl.BlockSpec(memory_space=pltpu.VMEM),
-    )(block_rows, block_cols, counts)
 
 
 def hand_over(src_a, src_b, src_c, dst_a, dst_b, dst_c):
@@ -268,9 +253,9 @@
 
 def fused_kernel(
     n_row, n_col, scale,
-    meta, features, weight, cotangent, values,
+    rows_ref, cols_ref, count_ref, features, weight, cotangent, values,
     out_ref, gw_ref, gf_ref,
-    vbuf, panel, cslab, slab, stage, acc, aggbuf, gfbuf, sib_in,
+    meta_v, meta, vbuf, panel, cslab, slab, stage, acc, aggbuf, gfbuf, sib_in,
     relay_l, relay_r, from_l, from_r, from_mate,
     crelay_l, crelay_r, cfrom_l, cfrom_r, cfrom_mate,
     agg, wterm, wsum, w1, w2, whalf,
@@ -343,12 +328,16 @@
     done = object()
     next(ag_c)
     next(ag_r)
+    sort_blocks(rows_ref, cols_ref, count_ref, meta_v)
+    load_meta = pltpu.make_async_copy(meta_v, meta, local_sem.at[3])
+    load_meta.start()
     for index in range(9):
         next(ag_c, done)
         if index >= 1:
             next(ag_r, done)
     drain(ag_c)
     load_values.wait()
+    load_meta.wait()
     acc[...] = jnp.zeros_like(acc)
     def forward(t, _):
         a, b = meta[0, BLK + 2 * t], meta[0, BLK + 2 * t + 1]
@@ -432,7 +421,7 @@
         copy.wait_send()
     for piece in range(13):
         lax.fori_loop(piece * UNROLL, (piece + 1) * UNROLL, backward, 0, unroll=UNROLL)
-        if piece in (0, 1, 2, 6, 7, 8, 9, 10, 12):
+        if piece in (0, 1, 2):
             drain(rs_r, 1)
     rs_c = scatter_steps(
         gfbuf, ring_c, rsc_s, rsc_r, crelay_l, crelay_r, cfrom_l, cfrom_r, cfrom_mate,
@@ -457,15 +446,18 @@
         _, device = chip(d)
         return remote(wsum.at[core, spot], wsum.at[core, spot], ws3_s, ws3_r, d - 1, device)
 
+    drain(rs_r, 2)
     drain(rs_c, 3)
+    drain(rs_r, 4)
     to_core = remote(wterm.at[1 - core], whalf, wc_s, wc_r, 0, sibling)
     to_core.start()
-    drain(rs_r, 1)
+    drain(rs_c, 2)
     to_core.wait_recv()
     wterm[core] = wterm[core] + whalf[...]
     for d in range(1, n_chip):
         w1_copy(d).start()
-    drain(rs_c, 5)
+    drain(rs_r, 1)
+    drain(rs_c, 3)
     drain(rs_r, 2)
     share = wterm[core, spot]
     for d in range(1, n_chip):
@@ -474,12 +466,7 @@
     w2[col] = share
     for d in range(1, n_col):
         w2_copy(d).start()
-    drain(rs_c, 2)
-    drain(rs_r)
-    for copy in swaps:
-        copy.wait_send()
-    for b in range(CHUNK):
-        out_ref[b] = jnp.dot(agg[b], weight[...], preferred_element_type=F32).astype(BF)
+    drain(rs_c, 1)
     for d in range(1, n_col):
         origin = (col + n_col - d) % n_col
         remote(w2.at[origin], w2.at[origin], ws2_s, ws2_r, d - 1, sibling).wait_recv()
@@ -489,7 +476,13 @@
     wsum[core, spot] = whole * scale
     for d in range(1, n_chip):
         w3_copy(d).start()
+    drain(rs_c, 1)
     drain(rs_c, 2)
+    drain(rs_r)
+    for copy in swaps:
+        copy.wait_send()
+    for b in range(CHUNK):
+        out_ref[b] = jnp.dot(agg[b], weight[...], preferred_element_type=F32).astype(BF)
     for d in range(1, n_chip):
         origin = (spot + n_chip - d) % n_chip
         remote(wsum.at[core, origin], wsum.at[core, origin], ws3_s, ws3_r, d - 1, sibling).wait_recv()
@@ -512,7 +505,6 @@
     n_col = lax.axis_size("col")
     width = features.shape[-1]
     nodes = features.shape[0] * n_row * n_col
-    meta = build_meta(block_rows[0], block_cols[0], counts)
     shard = (CHUNK, B, width)
 
     def vm(*shape, dtype=BF):
@@ -521,6 +513,7 @@
     dma = pltpu.SemaphoreType.DMA
     wide = (B, width)
     scratch = [
+        vm(1, 2 * META, dtype=jnp.int32), pltpu.SMEM((1, 2 * META), jnp.int32),
         vm(NNZ + 1, B, B), vm(CHUNK * n_col, *wide), vm(CHUNK * n_row, *wide), vm(CHUNK * n_row, *wide), vm(F_PAIRS, *wide),
         vm(*wide, dtype=F32), vm(CHUNK * n_row, *wide), vm(CHUNK * n_col, *wide), vm(CHUNK * n_row // 2, *wide),
         vm(2, 2, *wide), vm(2, 2, *wide), vm(2, CHUNK, *wide), vm(2, CHUNK, *wide), vm(*shard),
@@ -529,7 +522,7 @@
         vm(2, n_row // 2, width // n_row, width, dtype=F32), vm(2, n_row // 2, width // n_row, width, dtype=F32),
         vm(n_row // 2 - 1, width // n_row, width, dtype=F32), vm(n_col, width // n_row, width, dtype=F32),
         vm(n_row // 2, width // n_row, width, dtype=F32),
-        dma((3,)), dma((14,)), dma((14,)), dma((14,)), dma((14,)), dma((16,)), dma((16,)),
+        dma((4,)), dma((14,)), dma((14,)), dma((14,)), dma((14,)), dma((16,)), dma((16,)),
         dma((14,)), dma((14,)), dma((14,)), dma((14,)), dma((8,)), dma((8,)),
         dma((n_row // 2 - 1,)), dma((n_row // 2 - 1,)), dma((n_col - 1,)), dma((n_col - 1,)),
         dma((n_row // 2 - 1,)), dma((n_row // 2 - 1,)), dma((2,)), dma((2,)),
@@ -542,13 +535,13 @@
             jax.ShapeDtypeStruct((2, n_row // 2, width // n_row, width), F32),
             jax.ShapeDtypeStruct(shard, BF),
         ],
-        in_specs=[pl.BlockSpec(memory_space=pltpu.SMEM), pl.BlockSpec(memory_space=pl.ANY), vmem] + [pl.BlockSpec(memory_space=pl.ANY)] * 2,
+        in_specs=[vmem, vmem, pl.BlockSpec(memory_space=pltpu.SMEM), pl.BlockSpec(memory_space=pl.ANY), vmem] + [pl.BlockSpec(memory_space=pl.ANY)] * 2,
         out_specs=[vmem] * 3,
         scratch_shapes=scratch,
         compiler_params=pltpu.CompilerParams(
             collective_id=0, has_side_effects=True, vmem_limit_bytes=60 * 1024 * 1024
         ),
-    )(meta, features.reshape(shard), weight, cotangent.reshape(shard), values[0, 0])
+    )(block_rows[0], block_cols[0], counts, features.reshape(shard), weight, cotangent.reshape(shard), values[0, 0])
     out, gw, gf = pl.pallas_call(
         hand_over,
         out_shape=[jax.ShapeDtypeStruct(item.shape, item.dtype) for item in (out, gw, gf)],

time: 82.3 us -> 79.2 us (0.962); the launches traced: 82.1 us -> 78 us
  Pallas kernels: 80.8 us -> 76.7 us
    pallas_call x1 -> x0, Pallas kernels: 2.09 us -> none  [build_meta(): pl.pallas_call(meta_kernel, out_shape=jax.ShapeDtypeStruct((1, 2 * META),...]
    pallas_call x1, Pallas kernels: 76.7 us -> 74.7 us  [body(): pl.pallas_call(functools.partial(fused_kernel, n_row, n_col, float(nodes)...]
where the time goes in v3:
time: 79.2 us; the launch traced here: 78 us
  Pallas kernels  76.7 us (97%)
  between operations  1.29 us (2%)
    pallas_call x1, Pallas kernels, body(): pl.pallas_call(functools.partial(fused_kernel, n_row, n_col, float(nodes)...  74.7 us
    pallas_call x1, Pallas kernels, body(): pl.pallas_call(hand_over, out_shape=[jax.ShapeDtypeStruct(item.shape, ite...  2 us

profile of v3, /device:TPU:1, one launch (start us, length us, event | category | flops | bytes accessed | tf_op | source)
XLA Modules:
  0.0 78.0 jit_solution(10435411765449263526)
XLA Ops:
  1.3 74.7 %shard_map.94 = (bf16[4,128,256]{2,1,0:T(8,128)(2,1)}, f32[2,8,16,256]{3,2,1,0:T(8,128)}, bf16[4,128,256]{2,1,0:T(8,128)(2,1)}) custom-call(s32[1,384]{1,0:T(1,128)} %bitcast.11, s32[1,384]{1,0:T(1,128)} %bitcast.12, s32[1,1]{1,0:T(1,128)S(6)} %copy.10.count_ref, bf16[4,128,256]{2,1,0:T(8,128)(2,1)} %bitcast.9, bf16[256,256]{1,0:T(8,128)(2,1)} %weight.1, ...), custom_call_target="tpu_custom_call" | custom-call | tf_op jit(solution)/shard_map/pallas_call | solution.py:531
  76.0 2.0 %shard_map.95 = (bf16[4,128,256]{2,1,0:T(8,128)(2,1)}, f32[2,8,16,256]{3,2,1,0:T(8,128)}, bf16[4,128,256]{2,1,0:T(8,128)(2,1)}) custom-call(bf16[4,128,256]{2,1,0:T(8,128)(2,1)} %get-tuple-element.9.src_a, f32[2,8,16,256]{3,2,1,0:T(8,128)} %get-tuple-element.10.src_b, bf16[4,128,256]{2,1,0:T(8,128)(2,1)} %get-tuple-element.11.src_c), custom_call_target="tpu_custom_call" | custom-call | tf_op jit(solution)/shard_map/pallas_call | solution.py:545

commit v4 on v3

--- a/solution.py
+++ b/solution.py
@@ -376,14 +376,18 @@
 
     order = [(2, 1), (1, 1), (-1, 1), (2, 0), (1, 0), (-1, 0), (0, 1), (0, 0)]
     swaps = []
-    for m, (di, dj) in enumerate(order):
-        slot = ring_r.at(di, dj) + 1 - 2 * core
-        pick(aggbuf, slot, 0)
-        copy = remote(aggbuf.at[pl.ds(slot * CHUNK, CHUNK)], sib_in.at[pl.ds(m * CHUNK, CHUNK)], sx_s, sx_r, m, sibling)
-        copy.start()
-        swaps.append(copy)
-    for di, dj in order:
-        pick(aggbuf, ring_r.at(di, dj), 0)
+    for group in (order[:3], order[3:]):
+        for di, dj in group:
+            m = order.index((di, dj))
+            slot = ring_r.at(di, dj) + 1 - 2 * core
+            pick(aggbuf, slot, 0)
+            copy = remote(
+                aggbuf.at[pl.ds(slot * CHUNK, CHUNK)], sib_in.at[pl.ds(m * CHUNK, CHUNK)], sx_s, sx_r, m, sibling
+            )
+            copy.start()
+            swaps.append(copy)
+        for di, dj in group:
+            pick(aggbuf, ring_r.at(di, dj), 0)
 
     def ready_r(di, dj):
         m = order.index((di, dj))
@@ -420,9 +424,9 @@
     for copy in sib_taken:
         copy.wait_send()
     for piece in range(13):
-        lax.fori_loop(piece * UNROLL, (piece + 1) * UNROLL, backward, 0, unroll=UNROLL)
         if piece in (0, 1, 2):
             drain(rs_r, 1)
+        lax.fori_loop(piece * UNROLL, (piece + 1) * UNROLL, backward, 0, unroll=UNROLL)
     rs_c = scatter_steps(
         gfbuf, ring_c, rsc_s, rsc_r, crelay_l, crelay_r, cfrom_l, cfrom_r, cfrom_mate,
         lambda di, dj: pick(gfbuf, ring_c.at(di, dj), META), lambda di, dj: None, finish_c,
@@ -446,9 +450,8 @@
         _, device = chip(d)
         return remote(wsum.at[core, spot], wsum.at[core, spot], ws3_s, ws3_r, d - 1, device)
 
-    drain(rs_r, 2)
     drain(rs_c, 3)
-    drain(rs_r, 4)
+    drain(rs_r, 6)
     to_core = remote(wterm.at[1 - core], whalf, wc_s, wc_r, 0, sibling)
     to_core.start()
     drain(rs_c, 2)

time: 79.2 us -> 80.2 us (1.013)
  Pallas kernels: 76.7 us -> 77.8 us
    pallas_call x1, Pallas kernels: 74.7 us -> 75.8 us  [body(): pl.pallas_call(functools.partial(fused_kernel, n_row, n_col, float(nodes)...]
where the time goes in v4:
time: 80.2 us; the launch traced here: 79.1 us
  Pallas kernels  77.8 us (97%)
  between operations  1.29 us (2%)
    pallas_call x1, Pallas kernels, body(): pl.pallas_call(functools.partial(fused_kernel, n_row, n_col, float(nodes)...  75.8 us
    pallas_call x1, Pallas kernels, body(): pl.pallas_call(hand_over, out_shape=[jax.ShapeDtypeStruct(item.shape, ite...  2 us

profile of v4, /device:TPU:1, one launch (start us, length us, event | category | flops | bytes accessed | tf_op | source)
XLA Modules:
  0.0 79.1 jit_solution(18145260210821753804)
XLA Ops:
  1.3 75.8 %shard_map.94 = (bf16[4,128,256]{2,1,0:T(8,128)(2,1)}, f32[2,8,16,256]{3,2,1,0:T(8,128)}, bf16[4,128,256]{2,1,0:T(8,128)(2,1)}) custom-call(s32[1,384]{1,0:T(1,128)} %bitcast.11, s32[1,384]{1,0:T(1,128)} %bitcast.12, s32[1,1]{1,0:T(1,128)S(6)} %copy.10.count_ref, bf16[4,128,256]{2,1,0:T(8,128)(2,1)} %bitcast.9, bf16[256,256]{1,0:T(8,128)(2,1)} %weight.1, ...), custom_call_target="tpu_custom_call" | custom-call | tf_op jit(solution)/shard_map/pallas_call | solution.py:534
  77.1 2.0 %shard_map.95 = (bf16[4,128,256]{2,1,0:T(8,128)(2,1)}, f32[2,8,16,256]{3,2,1,0:T(8,128)}, bf16[4,128,256]{2,1,0:T(8,128)(2,1)}) custom-call(bf16[4,128,256]{2,1,0:T(8,128)(2,1)} %get-tuple-element.9.src_a, f32[2,8,16,256]{3,2,1,0:T(8,128)} %get-tuple-element.10.src_b, bf16[4,128,256]{2,1,0:T(8,128)(2,1)} %get-tuple-element.11.src_c), custom_call_target="tpu_custom_call" | custom-call | tf_op jit(solution)/shard_map/pallas_call | solution.py:548
